TPU v7x, 256 devices: a whole 4x4x8 slice. The times are simulated.
256 devices in a mesh: dp: 2 (over z_lo), seq: 128 (over y, z_hi, x, core).
Axes of the slice: x: 4, y: 4, z: 8 (z_hi: 4, z_lo: 2; z = z_hi * 2 + z_lo), core: 2. Of those that a mesh axis runs over, the one named last changes fastest.
Arguments:
- block_input: bfloat16 [2, 1024, 160, 256], P('dp', 'seq'), may hold values from -42 to 42
- cotangent: bfloat16 [2, 1024, 160, 256], P('dp', 'seq'), may hold values from -5.2 to 5.2
- group_norm_gain: float32 [256], replicated, may hold values from 0.5 to 2
- group_norm_bias: float32 [256], replicated, may hold values from -2 to 2
- w_spatial: bfloat16 [9, 256, 256], replicated, may hold values from -0.125 to 0.125
- w_temporal: bfloat16 [3, 256, 256], replicated, may hold values from -0.21875 to 0.21875
Outputs:
- block_grad: bfloat16 [2, 1024, 160, 256], P('dp', 'seq')
- spatial_grad: float32 [9, 256, 256], replicated
- temporal_grad: float32 [3, 256, 256], replicated
- gain_grad: float32 [256], replicated
- bias_grad: float32 [256], replicated
All inputs are finite; a program needn't handle non-finite values.
Results may differ from a plain program's by a relative error of at most 0.0051.
Values may be sent and summed in bfloat16 or wider, within the bound.
A program may use at most 64 MiB of HBM per device.

v0:
```python
import math

import jax
import jax.numpy as jnp
from jax import lax
from jax.sharding import PartitionSpec as P

NORM_GROUPS = 32
ROWS = 32


EPS = 1e-06


def with_halo(block, sides, width):
    for axis, dim in sides:
        count = lax.axis_size(axis)
        forward = [(i, i + 1) for i in range(count - 1)]
        forward.append((count - 1, 0))
        backward = [(target, source) for source, target in forward]
        low = lax.ppermute(
            lax.slice_in_dim(block, block.shape[dim] - width, None, axis=dim), axis, forward
        )
        high = lax.ppermute(lax.slice_in_dim(block, 0, width, axis=dim), axis, backward)
        block = jnp.concatenate([low, block, high], axis=dim)
    return block


def grouped_input(flat):
    return flat.reshape(flat.shape[0], NORM_GROUPS, -1)


def edge_rows(padded, place, slabs):
    row_count = padded.shape[0]
    row_ids = jnp.arange(row_count)
    dropped = (row_ids == 0) & (place == 0) | (row_ids == row_count - 1) & (place == slabs - 1)
    kept = jnp.where(dropped[:, None, None], jnp.zeros_like(padded), padded)
    return jnp.pad(kept, ((0, 0), (1, 1), (0, 0)))


def slab_taps(padded, row_count, col_count):
    width = padded.shape[-1]
    return [
        padded[dy : dy + row_count, dx : dx + col_count].reshape(row_count * col_count, width)
        for dy in range(3)
        for dx in range(3)
    ]


def temporal_grads(u_frames, g_frames, w_temporal):
    count_frames = u_frames.shape[0]
    width = u_frames.shape[2]
    grads = []
    back = None
    for k in range(3):
        early = u_frames[: count_frames - k].reshape(-1, width)
        late = g_frames[k:].reshape(-1, width)
        grads.append(
            lax.dot_general(
                early, late, (((0,), (0,)), ((), ())), preferred_element_type=jnp.float32
            )
        )
        term = lax.dot_general(
            late, w_temporal[k], (((1,), (1,)), ((), ())), preferred_element_type=jnp.float32
        )
        term = term.reshape(count_frames - k, -1, width)
        term = jnp.concatenate([term, jnp.zeros((k,) + term.shape[1:], term.dtype)], 0)
        back = term if k == 0 else back + term
    return (jnp.stack(grads), back)


def local(block_input, cotangent, group_norm_gain, group_norm_bias, w_spatial, w_temporal):
    x = block_input[0]
    grad_out = cotangent[0]
    rows_dev, col_count, channel_list = x.shape
    pixel_values = rows_dev * col_count
    slabs = ROWS // rows_dev
    offset = slabs // 2
    seq_count = lax.axis_size("seq")
    frame_count = seq_count // slabs
    index = lax.axis_index("seq")
    global_slab = lax.rem(index + offset, seq_count)
    place = lax.rem(global_slab, slabs)
    channels_per_group = channel_list // NORM_GROUPS
    count = frame_count * ROWS * col_count * channels_per_group
    weight_scale = 1.0 / math.sqrt(lax.axis_size("dp") * frame_count * ROWS * col_count)
    input_float = grouped_input(x.astype(jnp.float32).reshape(pixel_values, channel_list))
    total, square = lax.psum(
        (jnp.sum(input_float, axis=(0, 2)), jnp.sum(input_float * input_float, axis=(0, 2))), "seq"
    )
    group_mean = total / count
    inverse_deviation = lax.rsqrt(square / count - group_mean * group_mean + EPS)
    normalized_input = (
        (input_float - group_mean[None, :, None]) * inverse_deviation[None, :, None]
    ).reshape(pixel_values, channel_list)
    preactivation = normalized_input * group_norm_gain + group_norm_bias
    sigma = jax.nn.sigmoid(preactivation)
    act = (preactivation * sigma).astype(jnp.bfloat16).reshape(rows_dev, col_count, channel_list)
    act_ext = edge_rows(with_halo(act, (("seq", 0),), 1), place, slabs)
    act_taps = slab_taps(act_ext, rows_dev, col_count)
    conv_out = jnp.dot(act_taps[0], w_spatial[0], preferred_element_type=jnp.float32)
    for tap in range(1, 9):
        conv_out = conv_out + jnp.dot(
            act_taps[tap], w_spatial[tap], preferred_element_type=jnp.float32
        )
    conv_out = conv_out.astype(jnp.bfloat16)
    grad_flat = grad_out.reshape(pixel_values, channel_list)
    piece = pixel_values // seq_count
    moved_out, moved_grad = (
        lax.all_to_all(conv_out, "seq", split_axis=0, concat_axis=0, tiled=True),
        lax.all_to_all(grad_flat, "seq", split_axis=0, concat_axis=0, tiled=True),
    )
    ordered_out = jnp.roll(moved_out.reshape(seq_count, piece, channel_list), offset, axis=0)
    ordered_grad = jnp.roll(moved_grad.reshape(seq_count, piece, channel_list), offset, axis=0)
    temporal_part, back = temporal_grads(
        ordered_out.reshape(frame_count, slabs * piece, channel_list),
        ordered_grad.reshape(frame_count, slabs * piece, channel_list),
        w_temporal,
    )
    back_sent = jnp.roll(
        back.astype(jnp.bfloat16).reshape(seq_count, piece, channel_list), -offset, axis=0
    )
    conv_grad = lax.all_to_all(
        back_sent.reshape(pixel_values, channel_list),
        "seq",
        split_axis=0,
        concat_axis=0,
        tiled=True,
    )
    grad_ext = edge_rows(
        with_halo(conv_grad.reshape(rows_dev, col_count, channel_list), (("seq", 0),), 1),
        place,
        slabs,
    )
    grad_taps = slab_taps(grad_ext, rows_dev, col_count)
    act_grad = lax.dot_general(
        grad_taps[0], w_spatial[8], (((1,), (1,)), ((), ())), preferred_element_type=jnp.float32
    )
    for tap in range(1, 9):
        act_grad = act_grad + lax.dot_general(
            grad_taps[tap],
            w_spatial[8 - tap],
            (((1,), (1,)), ((), ())),
            preferred_element_type=jnp.float32,
        )
    spatial_part = jnp.stack(
        [
            lax.dot_general(
                act_taps[tap],
                conv_grad,
                (((0,), (0,)), ((), ())),
                preferred_element_type=jnp.float32,
            )
            for tap in range(9)
        ]
    )
    preactivation_gradient = act_grad * sigma * (1.0 + preactivation * (1.0 - sigma))
    gain_share = jnp.sum(preactivation_gradient * normalized_input, axis=0)
    bias_part = jnp.sum(preactivation_gradient, axis=0)
    norm_grad = grouped_input(preactivation_gradient * group_norm_gain)
    input_grouped = grouped_input(normalized_input)
    first, second = lax.psum(
        (jnp.sum(norm_grad, axis=(0, 2)), jnp.sum(norm_grad * input_grouped, axis=(0, 2))), "seq"
    )
    first = first / count
    second = second / count
    input_grad = inverse_deviation[None, :, None] * (
        norm_grad - first[None, :, None] - input_grouped * second[None, :, None]
    )
    block_grad = (
        grad_flat.astype(jnp.float32) + input_grad.reshape(pixel_values, channel_list)
    ).astype(jnp.bfloat16)
    block_grad = block_grad.reshape(1, rows_dev, col_count, channel_list)
    spatial_part, temporal_part, gain_share, bias_part = lax.psum(
        (spatial_part, temporal_part, gain_share, bias_part), ("dp", "seq")
    )
    return (
        block_grad,
        spatial_part * weight_scale,
        temporal_part * weight_scale,
        gain_share * weight_scale,
        bias_part * weight_scale,
    )


def solution(mesh):
    return jax.shard_map(
        local,
        mesh=mesh,
        in_specs=(P("dp", "seq", None, None), P("dp", "seq", None, None), P(), P(), P(), P()),
        out_specs=(P("dp", "seq", None, None), P(), P(), P(), P()),
        check_vma=False,
    )
```

profile of v0, /device:TPU:1, one launch (start us, length us, event | category | flops | bytes accessed | tf_op | source)
XLA Modules:
  0.0 1150.8 jit_solution(1291954888050345364)
XLA Ops:
  7.2 1.3 all_to_all.18
  8.4 46.7 %all_to_all.27 = bf16[128,10,256]{2,1,0:T(8,128)(2,1)S(1)} all-to-all(bf16[128,10,256]{2,1,0:T(8,128)(2,1)S(1)} %all_to_all.18), channel_id=1, replica_groups=mesh['dp'=2,'seq'=128] {'seq'}, dimensions={0} | all-to-all | bytes 1310720 | tf_op jit(solution)/shard_map/all_to_all | solution.py:111
  58.5 1.3 fusion.54
  59.8 1.3 fusion.56
  61.3 1.4 copy.24
  62.6 2.1 dot_general.105
  64.7 2.3 fusion.4
  67.0 1.3 reshape.189
  69.5 7.9 all-to-all-start.1
  78.1 362.0 %all-reduce.7 = (f32[32]{0:T(128)S(1)}, f32[32]{0:T(128)S(1)}) all-reduce(f32[32]{0:T(128)S(1)} %reduce_sum.73, f32[32]{0:T(128)S(1)} %reduce_sum.67), channel_id=1, replica_groups=mesh['dp'=2,'seq'=128] {'seq'}, use_global_device_ids=true, to_apply=%region_5.6 | all-reduce | flops 64 | bytes 512 | tf_op jit(solution)/shard_map/psum | solution.py:88
  443.8 1.9 collective-permute-done.1
  451.1 2.7 multiply_reduce_fusion
  456.7 350.6 %all-reduce.6 = (f32[32]{0:T(128)S(1)}, f32[32]{0:T(128)S(1)}) all-reduce(f32[32]{0:T(128)} %reduce_sum.93, f32[32]{0:T(128)} %reduce_sum.90), channel_id=1, replica_groups=mesh['dp'=2,'seq'=128] {'seq'}, use_global_device_ids=true, to_apply=%region_11.12 | all-reduce | flops 64 | bytes 512 | tf_op jit(solution)/shard_map/psum | solution.py:162
  809.9 3.2 multiply_convert_fusion.1
  814.5 1.3 multiply_convert_fusion
  824.2 2.1 all_to_all.22
  826.3 18.2 %all-to-all-start.2 = ((bf16[128,10,256]{2,1,0:T(8,128)(2,1)}), bf16[128,10,256]{2,1,0:T(8,128)(2,1)S(1)}, u32[]{:S(2)}, u32[]{:S(2)}) async-start(bf16[128,10,256]{2,1,0:T(8,128)(2,1)} %all_to_all.22), calls=%async_computation.2 | async-start | bytes 2097152 | tf_op jit(solution)/shard_map/all_to_all | solution.py:110
  844.6 2.3 fusion.18
  846.9 2.2 fusion.17
  856.7 19.3 %all-to-all-done.2 = bf16[128,10,256]{2,1,0:T(8,128)(2,1)S(1)} async-done(((bf16[128,10,256]{2,1,0:T(8,128)(2,1)}), bf16[128,10,256]{2,1,0:T(8,128)(2,1)S(1)}, u32[]{:S(2)}, u32[]{:S(2)}) %all-to-all-start.2) | async-done | bytes 655392 | tf_op jit(solution)/shard_map/all_to_all | solution.py:110
  877.4 2.0 convolution_bitcast_fusion.1
  882.3 72.9 %all-reduce.4 = (f32[256]{0:T(256)S(1)}, f32[256]{0:T(256)S(1)}) all-reduce(f32[256]{0:T(256)S(1)} %copy-done.36, f32[256]{0:T(256)S(1)} %copy-done.37), channel_id=1, replica_groups=mesh['dp'=2,'seq'=128] {'dp','seq'}, use_global_device_ids=true, to_apply=%region_15.16 | all-reduce | flops 512 | bytes 4096 | tf_op jit(solution)/shard_map/psum | solution.py:174
  955.8 183.9 %all-reduce.10.cloned.1.call-done = (f32[9,256,256]{2,1,0:T(8,128)}, f32[3,256,256]{2,1,0:T(8,128)}) async-done(((f32[9,256,256]{2,1,0:T(8,128)}, f32[3,256,256]{2,1,0:T(8,128)}), (f32[9,256,256]{2,1,0:T(8,128)}, f32[3,256,256]{2,1,0:T(8,128)})) %all-reduce.10.cloned.1.call-update) | async-done | bytes 3145744 | tf_op jit(solution)/shard_map/psum | solution.py:174
  1139.6 3.3 broadcast_multiply_fusion
  (162 shorter events, 42.7 us)
Async XLA Ops:
  69.5 7.9 copy-start
  69.5 372.2 %all-to-all-start.1 = ((bf16[128,10,256]{2,1,0:T(8,128)(2,1)}), bf16[128,10,256]{2,1,0:T(8,128)(2,1)S(1)}, u32[]{:S(2)}, u32[]{:S(2)}) async-start(bf16[128,10,256]{2,1,0:T(8,128)(2,1)} %pad_maximum_fusion), calls=%async_computation.1 | async-start | bytes 2097152 | tf_op jit(solution)/shard_map/all_to_all | solution.py:123
  440.3 9.9 copy-start.26
  440.5 9.8 copy-start.28
  441.8 3.9 collective-permute-start.1
  442.9 2.8 collective-permute-start
  809.8 4.6 copy-start.27
  809.8 4.6 copy-start.29
  809.9 4.6 copy-start.31
  809.9 4.6 copy-start.33
  813.7 3.1 collective-permute-start.2
  813.7 4.2 copy-start.35
  813.7 4.2 collective-permute-start.3
  815.8 2.2 copy-start.22
  819.8 2.5 copy-start.9
  819.8 2.8 copy-start.7
  819.8 3.2 copy-start.5
  826.3 49.7 %all-to-all-start.2 = ((bf16[128,10,256]{2,1,0:T(8,128)(2,1)}), bf16[128,10,256]{2,1,0:T(8,128)(2,1)S(1)}, u32[]{:S(2)}, u32[]{:S(2)}) async-start(bf16[128,10,256]{2,1,0:T(8,128)(2,1)} %all_to_all.22), calls=%async_computation.2 | async-start | bytes 2097152 | tf_op jit(solution)/shard_map/all_to_all | solution.py:110
  844.5 4.6 copy-start.18
  844.5 295.1 %all-reduce.10.cloned.1.call-start = ((), (), s32[]{:S(2)}) async-start(), calls=%async_computation.3 | async-start | bytes 6291456 | tf_op jit(solution)/shard_map/psum | solution.py:174
  844.6 2.3 copy-start.20
  844.6 4.5 copy-start.25
  846.9 3.3 copy-start.16
  1139.6 3.4 copy-start.24
  (21 other events, 32.0 us)
Sparse Core Ops, SparseCore 0:
  881.9 257.7 all-reduce.9
where the time goes:
time: 1150 us
  blocking collectives  832 us (72%)
  waiting for transfers between devices  206 us (18%)
  matrix products  29.8 us (3%)
  starting transfers between devices  28.7 us (2%)
  local copies, waits for them, and re-layouts  23 us (2%)
  other arithmetic  16.3 us (1%)
  between operations  14.6 us (1%)
    psum x1, blocking collectives, local(): lax.psum((jnp.sum(input_float, axis=(0, 2)), jnp.sum(input_float * input_...  362 us
    psum x1, blocking collectives, local(): lax.psum((jnp.sum(norm_grad, axis=(0, 2)), jnp.sum(norm_grad * input_grou...  351 us
    psum x1, waiting for transfers between devices, local(): lax.psum((spatial_part, temporal_part, gain_share, bias_part), ('dp', 'se...  184 us
    psum x1, blocking collectives, local(): lax.psum((spatial_part, temporal_part, gain_share, bias_part), ('dp', 'se...  72.9 us
    all_to_all x1, blocking collectives, local(): lax.all_to_all(grad_flat, 'seq', split_axis=0, concat_axis=0, tiled=True)  46.7 us
  transfers between devices with their start and end apart: 7, of which 4 were waited for; matrix products, arithmetic and copies ran while one was open for 1% of the time, Pallas kernels for 0%

commit v1 on v0

v1 whole, which is shorter than its diff:
```python
import math

import jax
import jax.numpy as jnp
from jax import lax
from jax.experimental import pallas as pl
from jax.experimental.pallas import tpu as pltpu
from jax.sharding import PartitionSpec as P

F32 = jnp.float32
BF16 = jnp.bfloat16
MESH = pl.DeviceIdType.MESH

CHANNELS = 256
GROUP = 8
ROWS_DEV = 8
COLS = 160
PIXELS = ROWS_DEV * COLS
PADDED = PIXELS + 2 * COLS
SEQ = 128
FRAMES = 32
EPS = 1e-06
COUNT = FRAMES * 32 * COLS * GROUP
SCALE = 1.0 / math.sqrt(2 * FRAMES * 32 * COLS)

ORDER = (0, 7, 1, 2, 3, 4, 5, 6)
BLOCK = 2 * COLS

TAPS = 12
HALF_ROWS = TAPS * CHANNELS
PART = HALF_ROWS // 2
QUARTER = PART // 4
SIXTEENTH = PART // 16
SHARD = 2 * SIXTEENTH // 4


def kernel(
    x_hbm, g_hbm, gain_ref, bias_ref, wsp_hbm, wt_hbm,
    grad_out, params_out, gain_out, bias_out,
    xv, cots, act3, act3t, cg3, conv, convt, wsp, wspt, wt, wtt, pre_grad,
    act_halo, cg_halo, stat_a, stat_b, back_a, back_b, clip_sums,
    part, core_in, in1a, in1b, mid_a, mid_b, in2a, in2b, mid2, in3, full,
    load_sem, far_send, far_recv, near_send, near_recv,
    ah_send, ah_recv, ch_send, ch_recv,
    sa_send, sa_recv, sb_send, sb_recv, ba_send, ba_recv, bb_send, bb_recv, clip_sem,
    core_send, core_recv, s1_send, s1_recv, s2_send, s2_recv, s3_send, s3_recv,
    g3_send, g3_recv, g2_send, g2_recv, g1_send, g1_recv, gc_send, gc_recv,
):
    clip = lax.axis_index("dp")
    seq = lax.axis_index("seq")
    core = lax.rem(seq, 2)
    x = lax.rem(seq // 2, 4)
    zh = lax.rem(seq // 8, 4)
    y = seq // 32
    low = lax.rem(seq, 8)
    high = seq // 8
    z = zh * 2 + clip
    slab = lax.rem(seq + 2, SEQ)
    place = lax.rem(slab, 4)
    frame = slab // 4

    def at(s):
        return (clip, s)

    def at_x(o):
        return (clip, seq + 2 * (o - x))

    def at_y(o):
        return (clip, seq + 32 * (o - y))

    def at_zh(o):
        return (clip, seq + 8 * (o - zh))

    def at_z(o):
        return (lax.rem(o, 2), seq + 8 * (o // 2 - zh))

    up = lax.rem(seq + 1, SEQ)
    down = lax.rem(seq + SEQ - 1, SEQ)
    far_to = lax.rem(seq + SEQ - 8, SEQ)
    far_from = lax.rem(seq + 8, SEQ)
    other_core = seq + 1 - 2 * core
    x_high = x // 2
    near_to = seq + 4 - 8 * x_high

    def copy(src, dst, send_sem, recv_sem, device):
        return pltpu.make_async_remote_copy(
            src_ref=src, dst_ref=dst, send_sem=send_sem, recv_sem=recv_sem,
            device_id=device, device_id_type=MESH,
        )

    load_x = pltpu.make_async_copy(x_hbm, xv, load_sem.at[0])
    load_g = pltpu.make_async_copy(g_hbm, cots.at[0], load_sem.at[1])
    load_wsp = pltpu.make_async_copy(wsp_hbm, wsp, load_sem.at[2])
    load_wt = pltpu.make_async_copy(wt_hbm, wt, load_sem.at[3])
    load_x.start()
    load_g.start()
    load_wsp.start()
    load_wt.start()

    barrier = pltpu.get_barrier_semaphore()

    def greet(device):
        pl.semaphore_signal(barrier, inc=1, device_id=device, device_id_type=MESH)

    def greet_low(j, _):
        greet(at(seq - low + lax.rem(low + j, 8)))
        return 0

    def greet_high(j, _):
        greet(at(lax.rem(high + j, 16) * 8 + low))
        return 0

    def greet_z(j, _):
        greet((1 - clip, seq + 8 * (j - zh)))
        return 0

    lax.fori_loop(1, 8, greet_low, 0)
    lax.fori_loop(1, 16, greet_high, 0)
    lax.fori_loop(0, 4, greet_z, 0)
    greet(at(up))
    greet(at(down))
    pl.semaphore_wait(barrier, 7 + 15 + 4 + 2)

    def far_copy(k):
        rows = pl.ds(ORDER[k] * COLS, COLS)
        return copy(
            g_hbm.at[rows], cots.at[2, rows], far_send.at[k], far_recv.at[k], at(far_to)
        )

    def near_copy(k):
        rows = pl.ds(ORDER[k] * COLS, COLS)
        return copy(
            cots.at[2 * (1 - x_high), rows], cots.at[1, rows],
            near_send.at[k], near_recv.at[k], at(near_to),
        )

    for k in range(8):
        far_copy(k).start()

    def exchange(buf, n, me, target, send_sem, recv_sem):
        def body(j, _):
            o = lax.rem(me + j, n)
            copy(buf.at[me], buf.at[me], send_sem.at[o], recv_sem.at[me], at(target(o))).start()
            return 0

        lax.fori_loop(1, n, body, 0)

    def collect(buf, n, me, target, send_sem, recv_sem):
        def body(j, _):
            o = lax.rem(me + j, n)
            arrived = copy(buf.at[o], buf.at[o], send_sem.at[o], recv_sem.at[o], at(target(o)))
            arrived.wait_send()
            arrived.wait_recv()
            return 0

        lax.fori_loop(1, n, body, 0)
        total = buf[0]
        for o in range(1, n):
            total = total + buf[o]
        return total

    def low_of(o):
        return seq - low + o

    def high_of(o):
        return o * 8 + low

    row_id = lax.broadcasted_iota(jnp.int32, (8, CHANNELS), 0)

    def pack_rows(first, second):
        return jnp.where(row_id == 0, first, jnp.where(row_id == 1, second, 0.0))

    group_a = lax.shift_right_logical(lax.broadcasted_iota(jnp.int32, (CHANNELS, CHANNELS), 0), 3)
    group_b = lax.shift_right_logical(lax.broadcasted_iota(jnp.int32, (CHANNELS, CHANNELS), 1), 3)
    same_group = jnp.where(group_a == group_b, 1.0, 0.0).astype(BF16)

    def group_sum(v):
        total = jnp.zeros_like(v)
        rest = v
        for _ in range(3):
            piece = rest.astype(BF16)
            rest = rest - piece.astype(F32)
            total = total + jnp.dot(piece, same_group, preferred_element_type=F32)
        return total

    load_x.wait()

    def stat_body(i, carry):
        a, b = carry
        blk = xv[pl.ds(i * COLS, COLS), :].astype(F32).reshape(COLS // 8, 8, CHANNELS)
        return a + jnp.sum(blk, axis=0), b + jnp.sum(blk * blk, axis=0)

    zero8 = jnp.zeros((8, CHANNELS), F32)
    a, b = lax.fori_loop(0, ROWS_DEV, stat_body, (zero8, zero8))
    stat_a[low] = pack_rows(jnp.sum(a, axis=0, keepdims=True), jnp.sum(b, axis=0, keepdims=True))
    exchange(stat_a, 8, low, low_of, sa_send, sa_recv)

    load_wt.wait()
    load_wsp.wait()
    for k in range(3):
        wtt[k] = wt[k].T

    def turn_weight(i, _):
        wspt[pl.ds(i * CHANNELS, CHANNELS), :] = wsp[pl.ds((8 - i) * CHANNELS, CHANNELS), :].T
        return 0

    lax.fori_loop(0, 9, turn_weight, 0)

    stat_b[high] = collect(stat_a, 8, low, low_of, sa_send, sa_recv)
    exchange(stat_b, 16, high, high_of, sb_send, sb_recv)
    load_g.wait()
    moments = group_sum(collect(stat_b, 16, high, high_of, sb_send, sb_recv)) * (1.0 / COUNT)
    mean = moments[0:1]
    rstd = lax.rsqrt(moments[1:2] - mean * mean + EPS)
    gain = gain_ref[...]
    bias = bias_ref[...]

    def forward(k):
        far_copy(k).wait_recv()
        near_copy(k).start()

    forward(0)
    forward(1)

    col_id = lax.broadcasted_iota(jnp.int32, (COLS, CHANNELS), 0)

    def store_shifts(buf, padded_row, v):
        rows = pl.ds(padded_row * COLS, COLS)
        buf[rows, CHANNELS : 2 * CHANNELS] = v.astype(BF16)
        left = jnp.where(col_id == 0, 0.0, pltpu.roll(v, 1, 0))
        right = jnp.where(col_id == COLS - 1, 0.0, pltpu.roll(v, COLS - 1, 0))
        buf[rows, 0:CHANNELS] = left.astype(BF16)
        buf[rows, 2 * CHANNELS : 3 * CHANNELS] = right.astype(BF16)

    def normalize(rows):
        xhat = (xv[rows, :].astype(F32) - mean) * rstd
        pre = xhat * gain + bias
        return xhat, pre, jax.nn.sigmoid(pre)

    def act_row(r):
        _, pre, sigma = normalize(pl.ds(r * COLS, COLS))
        store_shifts(act3, r + 1, pre * sigma)

    middle = slice(CHANNELS, 2 * CHANNELS)

    def halo_copies(buf, halo, send_sem, recv_sem):
        first = copy(
            buf.at[pl.ds(COLS, COLS), middle], halo.at[1], send_sem.at[0], recv_sem.at[1], at(down)
        )
        last = copy(
            buf.at[pl.ds(PIXELS, COLS), middle], halo.at[0], send_sem.at[1], recv_sem.at[0], at(up)
        )
        return first, last

    def send_halo(buf, halo, send_sem, recv_sem):
        for c in halo_copies(buf, halo, send_sem, recv_sem):
            c.start()

    def take_halo(buf, halo, send_sem, recv_sem):
        for c in halo_copies(buf, halo, send_sem, recv_sem):
            c.wait_send()
            c.wait_recv()
        keep_low = jnp.where(place > 0, 1.0, 0.0).astype(F32)
        keep_high = jnp.where(place < 3, 1.0, 0.0).astype(F32)
        store_shifts(buf, 0, halo[0].astype(F32) * keep_low)
        store_shifts(buf, ROWS_DEV + 1, halo[1].astype(F32) * keep_high)

    act_row(0)
    act_row(ROWS_DEV - 1)
    send_halo(act3, act_halo, ah_send, ah_recv)

    def act_body(r, _):
        act_row(r)
        return 0

    lax.fori_loop(1, ROWS_DEV - 1, act_body, 0)
    take_halo(act3, act_halo, ah_send, ah_recv)
    forward(2)

    def convolve(buf, weights, i):
        total = None
        for dy in range(3):
            term = jnp.dot(
                buf[pl.ds(i * BLOCK + dy * COLS, BLOCK), :],
                weights[dy * 3 * CHANNELS : (dy + 1) * 3 * CHANNELS, :],
                preferred_element_type=F32,
            )
            total = term if total is None else total + term
        return total

    def conv_body(i, _):
        conv[pl.ds(i * BLOCK, BLOCK), :] = convolve(act3, wsp, i).astype(BF16)
        return 0

    lax.fori_loop(0, PIXELS // BLOCK, conv_body, 0)
    forward(3)

    def turn_conv(i, _):
        src = pl.ds(pl.multiple_of(i * 128, 128), 128)
        convt[:, src] = conv[src, :].T
        return 0

    lax.fori_loop(0, PIXELS // 128, turn_conv, 0)

    for dy in range(3):
        def turn_act(i, _):
            dst = pl.ds(pl.multiple_of(i * 128, 128), 128)
            src = pl.ds(pl.multiple_of(dy * COLS + i * 128, 32), 128)
            act3t[dy, :, dst] = act3[src, :].T
            return 0

        lax.fori_loop(0, PIXELS // 128, turn_act, 0)
        forward(4 + dy)

    keep1 = jnp.where(frame < FRAMES - 1, 1.0, 0.0).astype(F32)
    keep2 = jnp.where(frame < FRAMES - 2, 1.0, 0.0).astype(F32)

    def cg_row(k):
        r = ORDER[k]
        near_copy(k).wait_recv()
        rows = pl.ds(r * COLS, COLS)
        total = jnp.dot(cots[0, rows, :], wtt[0], preferred_element_type=F32)
        total = total + keep1 * jnp.dot(cots[1, rows, :], wtt[1], preferred_element_type=F32)
        total = total + keep2 * jnp.dot(cots[2, rows, :], wtt[2], preferred_element_type=F32)
        store_shifts(cg3, r + 1, total.astype(BF16).astype(F32))

    for k in range(8):
        if k == 4:
            forward(7)
        cg_row(k)
        if k == 1:
            send_halo(cg3, cg_halo, ch_send, ch_recv)

    def put(first_row, v):
        part[0, pl.ds(first_row, v.shape[0]), :] = v[:, :128]
        part[1, pl.ds(first_row, v.shape[0]), :] = v[:, 128:]

    chunk_rows = 3 * CHANNELS

    def core_copy(i):
        rows = pl.ds(i * chunk_rows, chunk_rows)
        return copy(
            part.at[1 - core, rows], core_in.at[rows], core_send.at[i], core_recv.at[i],
            at(other_core),
        )

    for k, keep in enumerate((None, keep1, keep2)):
        v = jnp.dot(convt[...], cots[k], preferred_element_type=F32)
        put((9 + k) * CHANNELS, v if keep is None else v * keep)
    core_copy(3).start()
    for dy in range(3):
        put(
            dy * chunk_rows,
            jnp.dot(
                act3t[dy], cg3[COLS : COLS + PIXELS, middle], preferred_element_type=F32
            ),
        )
        core_copy(dy).start()

    take_halo(cg3, cg_halo, ch_send, ch_recv)

    def back_body(i, carry):
        rows = pl.ds(i * BLOCK, BLOCK)
        xhat, pre, sigma = normalize(rows)
        v = convolve(cg3, wspt, i) * sigma * (1.0 + pre * (1.0 - sigma))
        pre_grad[rows, :] = v
        a, b = carry
        a = a + jnp.sum(v.reshape(BLOCK // 8, 8, CHANNELS), axis=0)
        b = b + jnp.sum((v * xhat).reshape(BLOCK // 8, 8, CHANNELS), axis=0)
        return a, b

    a, b = lax.fori_loop(0, PIXELS // BLOCK, back_body, (zero8, zero8))
    back_a[low] = pack_rows(jnp.sum(a, axis=0, keepdims=True), jnp.sum(b, axis=0, keepdims=True))
    exchange(back_a, 8, low, low_of, ba_send, ba_recv)

    def add_core(i):
        core_copy(i).wait_send()
        core_copy(i).wait_recv()
        rows = pl.ds(i * chunk_rows, chunk_rows)
        part[core, rows, :] = part[core, rows, :] + core_in[rows, :]

    def loop3(me, body):
        def step(j, _):
            body(j, lax.rem(me + j, 4))
            return 0

        lax.fori_loop(1, 4, step, 0)

    def s1_copy(which, me, o, peer):
        buf = (in1a, in1b)[which]
        target = (at_x, at_y)[which]
        return copy(
            part.at[core, pl.ds(which * PART + o * QUARTER, QUARTER)], buf.at[me],
            s1_send.at[which, o], s1_recv.at[which, me], target(peer),
        )

    def s1_start(which):
        me = (x, y)[which]
        loop3(me, lambda j, o: s1_copy(which, me, o, o).start())

    add_core(3)
    add_core(2)
    s1_start(1)
    add_core(0)
    add_core(1)
    s1_start(0)

    back_b[high] = collect(back_a, 8, low, low_of, ba_send, ba_recv)
    exchange(back_b, 16, high, high_of, bb_send, bb_recv)

    def s1_finish(which):
        me = (x, y)[which]
        buf = (in1a, in1b)[which]
        mid = (mid_a, mid_b)[which]

        def wait(j, o):
            s1_copy(which, me, o, o).wait_send()
            s1_copy(which, o, o, o).wait_recv()

        loop3(me, wait)
        mine = pl.ds(which * PART + me * QUARTER, QUARTER)
        total = part[core, mine, :]
        for j in range(1, 4):
            total = total + buf[lax.rem(me + j, 4)]
        mid[...] = total

    def s2_copy(which, me, o):
        mid = (mid_a, mid_b)[which]
        buf = (in2a, in2b)[which]
        target = (at_y, at_x)[which]
        return copy(
            mid.at[pl.ds(o * SIXTEENTH, SIXTEENTH)], buf.at[me],
            s2_send.at[which, o], s2_recv.at[which, me], target(o),
        )

    def s2_start(which):
        me = (y, x)[which]
        loop3(me, lambda j, o: s2_copy(which, me, o).start())

    def s2_finish(which):
        me = (y, x)[which]
        mid = (mid_a, mid_b)[which]
        buf = (in2a, in2b)[which]

        def wait(j, o):
            s2_copy(which, me, o).wait_send()
            s2_copy(which, o, o).wait_recv()

        loop3(me, wait)
        total = mid[pl.ds(me * SIXTEENTH, SIXTEENTH), :]
        for j in range(1, 4):
            total = total + buf[lax.rem(me + j, 4)]
        mid2[which * SIXTEENTH : (which + 1) * SIXTEENTH, :] = total

    sums = collect(back_b, 16, high, high_of, bb_send, bb_recv)
    clip_sums[clip] = sums
    clip_copy = copy(
        clip_sums.at[clip], clip_sums.at[clip], clip_sem.at[0], clip_sem.at[1], (1 - clip, seq)
    )
    clip_copy.start()

    s1_finish(1)
    s2_start(1)
    s1_finish(0)
    s2_start(0)

    norm_sums = group_sum(sums * gain) * (1.0 / COUNT)
    m1 = norm_sums[0:1]
    m2 = norm_sums[1:2]

    def out_body(i, _):
        rows = pl.ds(i * COLS, COLS)
        xhat = (xv[rows, :].astype(F32) - mean) * rstd
        v = rstd * (pre_grad[rows, :] * gain - m1 - xhat * m2)
        grad_out[rows, :] = (cots[0, rows, :].astype(F32) + v).astype(BF16)
        return 0

    lax.fori_loop(0, ROWS_DEV, out_body, 0)

    s2_finish(1)
    s2_finish(0)

    def s3_copy(o, slot):
        return copy(
            mid2.at[pl.ds(SHARD * (o // 2), SHARD)], in3.at[slot],
            s3_send.at[o], s3_recv.at[slot], at_z(o),
        )

    def s3_start(j, _):
        s3_copy(lax.rem(z + j, 8), z).start()
        return 0

    def s3_wait(j, _):
        o = lax.rem(z + j, 8)
        s3_copy(o, z).wait_send()
        s3_copy(o, o).wait_recv()
        return 0

    lax.fori_loop(1, 8, s3_start, 0)
    in3[z] = mid2[pl.ds(SHARD * zh, SHARD), :]

    clip_copy.wait_send()
    copy(
        clip_sums.at[1 - clip], clip_sums.at[1 - clip], clip_sem.at[0], clip_sem.at[1],
        (1 - clip, seq),
    ).wait_recv()
    both = (clip_sums[0] + clip_sums[1]) * SCALE
    bias_out[...] = both[0:1]
    gain_out[...] = both[1:2]

    lax.fori_loop(1, 8, s3_wait, 0)
    total = in3[0]
    for o in range(1, 8):
        total = total + in3[o]

    def shard_at(o):
        second = o // 2
        first = 1 - second
        base = second * (PART + QUARTER * y + SIXTEENTH * x)
        base = base + first * (QUARTER * x + SIXTEENTH * y)
        return pl.multiple_of(base + SHARD * lax.rem(o, 2), SHARD)

    full[core, pl.ds(shard_at(zh), SHARD), :] = (total * SCALE).astype(BF16)

    def spread(where, me, target, send_sem, recv_sem, rows):
        def body(j, o):
            place_at = full.at[core, pl.ds(where(me), rows)]
            copy(place_at, place_at, send_sem.at[o], recv_sem.at[me], target(o)).start()

        loop3(me, body)

    def gather(where, me, target, send_sem, recv_sem, rows):
        def body(j, o):
            mine = full.at[core, pl.ds(where(me), rows)]
            theirs = full.at[core, pl.ds(where(o), rows)]
            copy(mine, mine, send_sem.at[o], recv_sem.at[me], target(o)).wait_send()
            copy(theirs, theirs, send_sem.at[o], recv_sem.at[o], target(o)).wait_recv()

        loop3(me, body)

    g3 = (shard_at, zh, at_zh, g3_send, g3_recv, SHARD)
    spread(*g3)
    gather(*g3)

    def sixteenth_a(o):
        return pl.multiple_of(QUARTER * x + SIXTEENTH * o, SIXTEENTH)

    def sixteenth_b(o):
        return pl.multiple_of(PART + QUARTER * y + SIXTEENTH * o, SIXTEENTH)

    def quarter_a(o):
        return pl.multiple_of(QUARTER * o, QUARTER)

    def quarter_b(o):
        return pl.multiple_of(PART + QUARTER * o, QUARTER)

    g2a = (sixteenth_a, y, at_y, g2_send.at[0], g2_recv.at[0], SIXTEENTH)
    g2b = (sixteenth_b, x, at_x, g2_send.at[1], g2_recv.at[1], SIXTEENTH)
    g1a = (quarter_a, x, at_x, g1_send.at[0], g1_recv.at[0], QUARTER)
    g1b = (quarter_b, y, at_y, g1_send.at[1], g1_recv.at[1], QUARTER)
    spread(*g2a)
    spread(*g2b)
    gather(*g2a)
    spread(*g1a)
    gather(*g2b)
    spread(*g1b)

    def to_core(i, half):
        rows = full.at[half, pl.ds(i * PART, PART)]
        return copy(rows, rows, gc_send.at[i], gc_recv.at[i], at(other_core))

    gather(*g1a)
    to_core(0, core).start()
    gather(*g1b)
    to_core(1, core).start()
    for i in range(2):
        to_core(i, core).wait_send()
        to_core(i, 1 - core).wait_recv()
    params_out[...] = full[...]

    for k in range(8):
        far_copy(k).wait_send()
        near_copy(k).wait_send()


def local(block_input, cotangent, group_norm_gain, group_norm_bias, w_spatial, w_temporal):
    any_space = pl.BlockSpec(memory_space=pl.ANY)
    vmem = pl.BlockSpec(memory_space=pltpu.VMEM)
    dma = pltpu.SemaphoreType.DMA
    scratch = [
        pltpu.VMEM((PIXELS, CHANNELS), BF16),
        pltpu.VMEM((3, PIXELS, CHANNELS), BF16),
        pltpu.VMEM((PADDED, 3 * CHANNELS), BF16),
        pltpu.VMEM((3, 3 * CHANNELS, PIXELS), BF16),
        pltpu.VMEM((PADDED, 3 * CHANNELS), BF16),
        pltpu.VMEM((PIXELS, CHANNELS), BF16),
        pltpu.VMEM((CHANNELS, PIXELS), BF16),
        pltpu.VMEM((9 * CHANNELS, CHANNELS), BF16),
        pltpu.VMEM((9 * CHANNELS, CHANNELS), BF16),
        pltpu.VMEM((3, CHANNELS, CHANNELS), BF16),
        pltpu.VMEM((3, CHANNELS, CHANNELS), BF16),
        pltpu.VMEM((PIXELS, CHANNELS), F32),
        pltpu.VMEM((2, COLS, CHANNELS), BF16),
        pltpu.VMEM((2, COLS, CHANNELS), BF16),
        pltpu.VMEM((8, 8, CHANNELS), F32),
        pltpu.VMEM((16, 8, CHANNELS), F32),
        pltpu.VMEM((8, 8, CHANNELS), F32),
        pltpu.VMEM((16, 8, CHANNELS), F32),
        pltpu.VMEM((2, 8, CHANNELS), F32),
        pltpu.VMEM((2, HALF_ROWS, 128), F32),
        pltpu.VMEM((HALF_ROWS, 128), F32),
        pltpu.VMEM((4, QUARTER, 128), F32),
        pltpu.VMEM((4, QUARTER, 128), F32),
        pltpu.VMEM((QUARTER, 128), F32),
        pltpu.VMEM((QUARTER, 128), F32),
        pltpu.VMEM((4, SIXTEENTH, 128), F32),
        pltpu.VMEM((4, SIXTEENTH, 128), F32),
        pltpu.VMEM((2 * SIXTEENTH, 128), F32),
        pltpu.VMEM((8, SHARD, 128), F32),
        pltpu.VMEM((2, HALF_ROWS, 128), BF16),
        dma((4,)),
        dma((8,)), dma((8,)), dma((8,)), dma((8,)),
        dma((2,)), dma((2,)), dma((2,)), dma((2,)),
        dma((8,)), dma((8,)), dma((16,)), dma((16,)),
        dma((8,)), dma((8,)), dma((16,)), dma((16,)),
        dma((2,)),
        dma((4,)), dma((4,)),
        dma((2, 4)), dma((2, 4)), dma((2, 4)), dma((2, 4)),
        dma((8,)), dma((8,)),
        dma((4,)), dma((4,)), dma((2, 4)), dma((2, 4)), dma((2, 4)), dma((2, 4)),
        dma((2,)), dma((2,)),
    ]
    grad, params, gain_grad, bias_grad = pl.pallas_call(
        kernel,
        out_shape=(
            jax.ShapeDtypeStruct((PIXELS, CHANNELS), BF16),
            jax.ShapeDtypeStruct((2, HALF_ROWS, 128), BF16),
            jax.ShapeDtypeStruct((1, CHANNELS), F32),
            jax.ShapeDtypeStruct((1, CHANNELS), F32),
        ),
        in_specs=[any_space, any_space, vmem, vmem, any_space, any_space],
        out_specs=(vmem, vmem, vmem, vmem),
        scratch_shapes=scratch,
        compiler_params=pltpu.CompilerParams(
            collective_id=0, has_side_effects=True, vmem_limit_bytes=56 * 2**20
        ),
    )(
        block_input.reshape(PIXELS, CHANNELS),
        cotangent.reshape(PIXELS, CHANNELS),
        group_norm_gain.reshape(1, CHANNELS),
        group_norm_bias.reshape(1, CHANNELS),
        w_spatial.reshape(9 * CHANNELS, CHANNELS),
        w_temporal,
    )
    params = params.reshape(2, TAPS, CHANNELS, 128).transpose(1, 2, 0, 3)
    params = params.reshape(TAPS, CHANNELS, CHANNELS).astype(F32)
    return (
        grad.reshape(1, ROWS_DEV, COLS, CHANNELS),
        params[:9],
        params[9:],
        gain_grad.reshape(CHANNELS),
        bias_grad.reshape(CHANNELS),
    )


def solution(mesh):
    return jax.shard_map(
        local,
        mesh=mesh,
        in_specs=(P("dp", "seq", None, None), P("dp", "seq", None, None), P(), P(), P(), P()),
        out_specs=(P("dp", "seq", None, None), P(), P(), P(), P()),
        check_vma=False,
    )
```

time: 1150 us -> 124 us (0.11)
  blocking collectives: 832 us -> 0 us
  waiting for transfers between devices: 206 us -> 0 us
  Pallas kernels: 0 us -> 117 us
  matrix products: 29.8 us -> 0 us
  starting transfers between devices: 28.7 us -> 0 us
  local copies, waits for them, and re-layouts: 23 us -> 4.53 us
  other arithmetic: 16.3 us -> 1.74 us
  between operations: 14.6 us -> 0.65 us
    psum x3 -> x0, blocking collectives: 785 us -> none  [the longest x1 362 us: local(): lax.psum((jnp.sum(input_float, axis=(0, 2)), jnp.sum(input_float * input_...]
    psum x1 -> x0, waiting for transfers between devices: 184 us -> none  [local(): lax.psum((spatial_part, temporal_part, gain_share, bias_part), ('dp', 'se...]
    pallas_call x0 -> x1, Pallas kernels: none -> 117 us  [local(): pl.pallas_call(kernel, out_shape=(jax.ShapeDtypeStruct((PIXELS, CHANNELS)...]
    all_to_all x1 -> x0, blocking collectives: 46.7 us -> none  [local(): lax.all_to_all(grad_flat, 'seq', split_axis=0, concat_axis=0, tiled=True)]
    dot_general x33 -> x0, matrix products: 29.8 us -> none  [the longest x9 12.1 us: local(): lax.dot_general(act_taps[tap], conv_grad, (((0,), (0,)), ((), ())), prefe...]
    all_to_all x2 -> x0, starting transfers between devices: 26.1 us -> none  [the longest x1 18.2 us: local(): lax.all_to_all(conv_out, 'seq', split_axis=0, concat_axis=0, tiled=True)]
    all_to_all x2 -> x0, waiting for transfers between devices: 19.3 us -> none  [the longest x1 19.3 us: local(): lax.all_to_all(conv_out, 'seq', split_axis=0, concat_axis=0, tiled=True)]
  transfers between devices with their start and end apart: 7 -> 0, of which waited for: 4 -> 0; matrix products, arithmetic and copies ran while one was open for 1% -> 0% of each run, Pallas kernels for 0% -> 0%
where the time goes in v1:
time: 124 us
  Pallas kernels  117 us (94%)
  local copies, waits for them, and re-layouts  4.53 us (4%)
  other arithmetic  1.74 us (1%)
    pallas_call x1, Pallas kernels, local(): pl.pallas_call(kernel, out_shape=(jax.ShapeDtypeStruct((PIXELS, CHANNELS)...  117 us

profile of v1, /device:TPU:1, one launch (start us, length us, event | category | flops | bytes accessed | tf_op | source)
XLA Modules:
  0.0 123.8 jit_solution(14635936361809601135)
XLA Ops:
  0.6 116.9 %shard_map.101 = (bf16[1280,256]{1,0:T(8,128)(2,1)}, bf16[2,3072,128]{2,1,0:T(8,128)(2,1)}, f32[1,256]{1,0:T(1,128)}, f32[1,256]{1,0:T(1,128)}) custom-call(bf16[1280,256]{1,0:T(8,128)(2,1)} %bitcast.25, bf16[1280,256]{1,0:T(8,128)(2,1)} %bitcast.26, f32[1,256]{1,0:T(1,128)} %bitcast.27, f32[1,256]{1,0:T(1,128)} %bitcast.28, bf16[2304,256]{1,0:T(8,128)(2,1)} %bitcast.23, ...), custom_call_target="tpu_custom_call" | custom-call | tf_op jit(solution)/shard_map/pallas_call | solution.py:633
  117.5 1.7 %convert_bitcast_fusion = f32[12,256,2,128]{3,1,0,2:T(8,128)S(1)} fusion(bf16[2,12,256,128]{3,2,1,0:T(8,128)(2,1)} %bitcast.22), kind=kLoop, calls=%fused_computation | loop fusion | flops 786432 | bytes 4718592 | tf_op jit(solution)/shard_map/convert_element_type | solution.py:656
  119.3 0.9 copy_bitcast_fusion.1
  120.2 0.0 copy-start
  120.2 0.0 copy-start.2
  120.2 0.0 copy-start.1
  120.2 1.6 %copy_bitcast_fusion = f32[9,256,256]{2,1,0:T(8,128)} fusion(f32[12,256,2,128]{3,1,0,2:T(8,128)S(1)} %convert_bitcast_fusion), kind=kLoop, calls=%fused_computation.1 | loop fusion | bytes 4718592 | tf_op jit(solution)/shard_map/slice | solution.py:659
  121.8 0.0 copy-done
  121.8 0.8 copy.20
  122.7 0.0 copy-done.2
  122.7 0.6 copy.21
  123.2 0.0 copy-done.1
  123.2 0.6 copy.22
Async XLA Ops:
  120.2 1.6 %copy-start = (bf16[1280,256]{1,0:T(8,128)(2,1)S(1)}, bf16[1280,256]{1,0:T(8,128)(2,1)}, u32[]{:S(2)}) copy-start(bf16[1280,256]{1,0:T(8,128)(2,1)} %get-tuple-element.9) | copy-start | bytes 1966084
  120.2 2.5 %copy-start.2 = (f32[1,256]{1,0:T(1,128)S(1)}, f32[1,256]{1,0:T(1,128)}, u32[]{:S(2)}) copy-start(f32[1,256]{1,0:T(1,128)} %get-tuple-element.11) | copy-start | bytes 3076
  120.2 3.0 %copy-start.1 = (f32[1,256]{1,0:T(1,128)S(1)}, f32[1,256]{1,0:T(1,128)}, u32[]{:S(2)}) copy-start(f32[1,256]{1,0:T(1,128)} %get-tuple-element.12) | copy-start | bytes 3076

commit v2 on v1

--- a/solution.py
+++ b/solution.py
@@ -37,9 +37,9 @@
 def kernel(
     x_hbm, g_hbm, gain_ref, bias_ref, wsp_hbm, wt_hbm,
     grad_out, params_out, gain_out, bias_out,
-    xv, cots, act3, act3t, cg3, conv, convt, wsp, wspt, wt, wtt, pre_grad,
+    xv, cots, act3, cg3, conv, convt, wsp, wspt, wt, wtt, pre_grad,
     act_halo, cg_halo, stat_a, stat_b, back_a, back_b, clip_sums,
-    part, core_in, in1a, in1b, mid_a, mid_b, in2a, in2b, mid2, in3, full,
+    part, core_in, in1a, in1b, mid_a, mid_b, in2a, in2b, mid2, in3, full, grad_v,
     load_sem, far_send, far_recv, near_send, near_recv,
     ah_send, ah_recv, ch_send, ch_recv,
     sa_send, sa_recv, sb_send, sb_recv, ba_send, ba_recv, bb_send, bb_recv, clip_sem,
@@ -127,15 +127,20 @@
             g_hbm.at[rows], cots.at[2, rows], far_send.at[k], far_recv.at[k], at(far_to)
         )
 
-    def near_copy(k):
+    def near_copy(k, own):
         rows = pl.ds(ORDER[k] * COLS, COLS)
         return copy(
-            cots.at[2 * (1 - x_high), rows], cots.at[1, rows],
+            (g_hbm if own else cots.at[2]).at[rows], cots.at[1, rows],
             near_send.at[k], near_recv.at[k], at(near_to),
         )
 
     for k in range(8):
         far_copy(k).start()
+
+    @pl.when(x_high == 1)
+    def send_own():
+        for k in range(8):
+            near_copy(k, True).start()
 
     def exchange(buf, n, me, target, send_sem, recv_sem):
         def body(j, _):
@@ -149,7 +154,6 @@
         def body(j, _):
             o = lax.rem(me + j, n)
             arrived = copy(buf.at[o], buf.at[o], send_sem.at[o], recv_sem.at[o], at(target(o)))
-            arrived.wait_send()
             arrived.wait_recv()
             return 0
 
@@ -158,6 +162,14 @@
         for o in range(1, n):
             total = total + buf[o]
         return total
+
+    def drain(buf, n, me, target, send_sem, recv_sem):
+        def body(j, _):
+            o = lax.rem(me + j, n)
+            copy(buf.at[me], buf.at[me], send_sem.at[o], recv_sem.at[me], at(target(o))).wait_send()
+            return 0
+
+        lax.fori_loop(1, n, body, 0)
 
     def low_of(o):
         return seq - low + o
@@ -217,10 +229,11 @@
 
     def forward(k):
         far_copy(k).wait_recv()
-        near_copy(k).start()
-
-    forward(0)
-    forward(1)
+
+        @pl.when(x_high == 0)
+        def pass_on():
+            near_copy(k, False).start()
+
 
     col_id = lax.broadcasted_iota(jnp.int32, (COLS, CHANNELS), 0)
 
@@ -258,7 +271,6 @@
 
     def take_halo(buf, halo, send_sem, recv_sem):
         for c in halo_copies(buf, halo, send_sem, recv_sem):
-            c.wait_send()
             c.wait_recv()
         keep_low = jnp.where(place > 0, 1.0, 0.0).astype(F32)
         keep_high = jnp.where(place < 3, 1.0, 0.0).astype(F32)
@@ -274,8 +286,9 @@
         return 0
 
     lax.fori_loop(1, ROWS_DEV - 1, act_body, 0)
+    forward(0)
     take_halo(act3, act_halo, ah_send, ah_recv)
-    forward(2)
+    forward(1)
 
     def convolve(buf, weights, i):
         total = None
@@ -293,7 +306,7 @@
         return 0
 
     lax.fori_loop(0, PIXELS // BLOCK, conv_body, 0)
-    forward(3)
+    forward(2)
 
     def turn_conv(i, _):
         src = pl.ds(pl.multiple_of(i * 128, 128), 128)
@@ -302,38 +315,41 @@
 
     lax.fori_loop(0, PIXELS // 128, turn_conv, 0)
 
-    for dy in range(3):
-        def turn_act(i, _):
-            dst = pl.ds(pl.multiple_of(i * 128, 128), 128)
-            src = pl.ds(pl.multiple_of(dy * COLS + i * 128, 32), 128)
-            act3t[dy, :, dst] = act3[src, :].T
-            return 0
-
-        lax.fori_loop(0, PIXELS // 128, turn_act, 0)
-        forward(4 + dy)
-
     keep1 = jnp.where(frame < FRAMES - 1, 1.0, 0.0).astype(F32)
     keep2 = jnp.where(frame < FRAMES - 2, 1.0, 0.0).astype(F32)
 
     def cg_row(k):
         r = ORDER[k]
-        near_copy(k).wait_recv()
+        near_copy(k, True).wait_recv()
         rows = pl.ds(r * COLS, COLS)
         total = jnp.dot(cots[0, rows, :], wtt[0], preferred_element_type=F32)
         total = total + keep1 * jnp.dot(cots[1, rows, :], wtt[1], preferred_element_type=F32)
         total = total + keep2 * jnp.dot(cots[2, rows, :], wtt[2], preferred_element_type=F32)
         store_shifts(cg3, r + 1, total.astype(BF16).astype(F32))
 
-    for k in range(8):
-        if k == 4:
-            forward(7)
-        cg_row(k)
-        if k == 1:
-            send_halo(cg3, cg_halo, ch_send, ch_recv)
-
-    def put(first_row, v):
-        part[0, pl.ds(first_row, v.shape[0]), :] = v[:, :128]
-        part[1, pl.ds(first_row, v.shape[0]), :] = v[:, 128:]
+    def put(first_row, v, add):
+        rows = pl.ds(first_row, v.shape[0])
+        for half in range(2):
+            w = v[:, half * 128 : (half + 1) * 128]
+            part[half, rows, :] = part[half, rows, :] + w if add else w
+
+    half_pixels = PIXELS // 2
+
+    def temporal_half(h):
+        pixels = slice(h * half_pixels, (h + 1) * half_pixels)
+        for k, keep in enumerate((None, keep1, keep2)):
+            v = jnp.dot(convt[:, pixels], cots[k, pixels, :], preferred_element_type=F32)
+            put((9 + k) * CHANNELS, v if keep is None else v * keep, h > 0)
+
+    def spatial_half(h, dy):
+        begin = h * half_pixels
+        v = lax.dot_general(
+            act3[dy * COLS + begin : dy * COLS + begin + half_pixels, :],
+            cg3[COLS + begin : COLS + begin + half_pixels, middle],
+            (((0,), (0,)), ((), ())),
+            preferred_element_type=F32,
+        )
+        put(dy * chunk_rows, v, h > 0)
 
     chunk_rows = 3 * CHANNELS
 
@@ -344,22 +360,31 @@
             at(other_core),
         )
 
-    for k, keep in enumerate((None, keep1, keep2)):
-        v = jnp.dot(convt[...], cots[k], preferred_element_type=F32)
-        put((9 + k) * CHANNELS, v if keep is None else v * keep)
+    forward(3)
+    cg_row(0)
+    cg_row(1)
+    send_halo(cg3, cg_halo, ch_send, ch_recv)
+    forward(4)
+    cg_row(2)
+    forward(5)
+    cg_row(3)
+    forward(6)
+    cg_row(4)
+    temporal_half(0)
+    forward(7)
+    for dy in range(3):
+        spatial_half(0, dy)
+    cg_row(5)
+    take_halo(cg3, cg_halo, ch_send, ch_recv)
+    cg_row(6)
+    cg_row(7)
+    temporal_half(1)
     core_copy(3).start()
-    for dy in range(3):
-        put(
-            dy * chunk_rows,
-            jnp.dot(
-                act3t[dy], cg3[COLS : COLS + PIXELS, middle], preferred_element_type=F32
-            ),
-        )
+    for dy in (0, 1, 2):
+        spatial_half(1, dy)
         core_copy(dy).start()
 
-    take_halo(cg3, cg_halo, ch_send, ch_recv)
-
-    def back_body(i, carry):
+    def back_block(i, carry):
         rows = pl.ds(i * BLOCK, BLOCK)
         xhat, pre, sigma = normalize(rows)
         v = convolve(cg3, wspt, i) * sigma * (1.0 + pre * (1.0 - sigma))
@@ -369,23 +394,6 @@
         b = b + jnp.sum((v * xhat).reshape(BLOCK // 8, 8, CHANNELS), axis=0)
         return a, b
 
-    a, b = lax.fori_loop(0, PIXELS // BLOCK, back_body, (zero8, zero8))
-    back_a[low] = pack_rows(jnp.sum(a, axis=0, keepdims=True), jnp.sum(b, axis=0, keepdims=True))
-    exchange(back_a, 8, low, low_of, ba_send, ba_recv)
-
-    def add_core(i):
-        core_copy(i).wait_send()
-        core_copy(i).wait_recv()
-        rows = pl.ds(i * chunk_rows, chunk_rows)
-        part[core, rows, :] = part[core, rows, :] + core_in[rows, :]
-
-    def loop3(me, body):
-        def step(j, _):
-            body(j, lax.rem(me + j, 4))
-            return 0
-
-        lax.fori_loop(1, 4, step, 0)
-
     def s1_copy(which, me, o, peer):
         buf = (in1a, in1b)[which]
         target = (at_x, at_y)[which]
@@ -394,16 +402,31 @@
             s1_send.at[which, o], s1_recv.at[which, me], target(peer),
         )
 
-    def s1_start(which):
+    def add_core(i):
+        core_copy(i).wait_recv()
+        rows = pl.ds(i * chunk_rows, chunk_rows)
+        part[core, rows, :] = part[core, rows, :] + core_in[rows, :]
+        which = i // 2
         me = (x, y)[which]
-        loop3(me, lambda j, o: s1_copy(which, me, o, o).start())
-
-    add_core(3)
-    add_core(2)
-    s1_start(1)
-    add_core(0)
-    add_core(1)
-    s1_start(0)
+        for o in (2 * (i % 2), 2 * (i % 2) + 1):
+            @pl.when(me != o)
+            def send_slice():
+                s1_copy(which, me, o, o).start()
+
+    sums = (zero8, zero8)
+    for i, chunk in enumerate((3, 0, 1, 2)):
+        sums = back_block(i, sums)
+        add_core(chunk)
+    a, b = sums
+    back_a[low] = pack_rows(jnp.sum(a, axis=0, keepdims=True), jnp.sum(b, axis=0, keepdims=True))
+    exchange(back_a, 8, low, low_of, ba_send, ba_recv)
+
+    def loop3(me, body):
+        def step(j, _):
+            body(j, lax.rem(me + j, 4))
+            return 0
+
+        lax.fori_loop(1, 4, step, 0)
 
     back_b[high] = collect(back_a, 8, low, low_of, ba_send, ba_recv)
     exchange(back_b, 16, high, high_of, bb_send, bb_recv)
@@ -414,7 +437,6 @@
         mid = (mid_a, mid_b)[which]
 
         def wait(j, o):
-            s1_copy(which, me, o, o).wait_send()
             s1_copy(which, o, o, o).wait_recv()
 
         loop3(me, wait)
@@ -443,7 +465,6 @@
         buf = (in2a, in2b)[which]
 
         def wait(j, o):
-            s2_copy(which, me, o).wait_send()
             s2_copy(which, o, o).wait_recv()
 
         loop3(me, wait)
@@ -451,6 +472,11 @@
         for j in range(1, 4):
             total = total + buf[lax.rem(me + j, 4)]
         mid2[which * SIXTEENTH : (which + 1) * SIXTEENTH, :] = total
+
+    s1_finish(1)
+    s2_start(1)
+    s1_finish(0)
+    s2_start(0)
 
     sums = collect(back_b, 16, high, high_of, bb_send, bb_recv)
     clip_sums[clip] = sums
@@ -458,12 +484,6 @@
         clip_sums.at[clip], clip_sums.at[clip], clip_sem.at[0], clip_sem.at[1], (1 - clip, seq)
     )
     clip_copy.start()
-
-    s1_finish(1)
-    s2_start(1)
-    s1_finish(0)
-    s2_start(0)
-
     norm_sums = group_sum(sums * gain) * (1.0 / COUNT)
     m1 = norm_sums[0:1]
     m2 = norm_sums[1:2]
@@ -472,13 +492,12 @@
         rows = pl.ds(i * COLS, COLS)
         xhat = (xv[rows, :].astype(F32) - mean) * rstd
         v = rstd * (pre_grad[rows, :] * gain - m1 - xhat * m2)
-        grad_out[rows, :] = (cots[0, rows, :].astype(F32) + v).astype(BF16)
+        grad_v[rows, :] = (cots[0, rows, :].astype(F32) + v).astype(BF16)
         return 0
 
     lax.fori_loop(0, ROWS_DEV, out_body, 0)
-
-    s2_finish(1)
-    s2_finish(0)
+    store_grad = pltpu.make_async_copy(grad_v, grad_out, load_sem.at[4])
+    store_grad.start()
 
     def s3_copy(o, slot):
         return copy(
@@ -486,20 +505,29 @@
             s3_send.at[o], s3_recv.at[slot], at_z(o),
         )
 
-    def s3_start(j, _):
-        s3_copy(lax.rem(z + j, 8), z).start()
-        return 0
+    def s3_start(which):
+        def body(j, _):
+            o = 4 * which + j
+
+            @pl.when(o != z)
+            def send_shard():
+                s3_copy(o, z).start()
+
+            return 0
+
+        lax.fori_loop(0, 4, body, 0)
 
     def s3_wait(j, _):
         o = lax.rem(z + j, 8)
-        s3_copy(o, z).wait_send()
         s3_copy(o, o).wait_recv()
         return 0
 
-    lax.fori_loop(1, 8, s3_start, 0)
+    s2_finish(1)
+    s3_start(1)
+    s2_finish(0)
+    s3_start(0)
     in3[z] = mid2[pl.ds(SHARD * zh, SHARD), :]
 
-    clip_copy.wait_send()
     copy(
         clip_sums.at[1 - clip], clip_sums.at[1 - clip], clip_sem.at[0], clip_sem.at[1],
         (1 - clip, seq),
@@ -531,9 +559,7 @@
 
     def gather(where, me, target, send_sem, recv_sem, rows):
         def body(j, o):
-            mine = full.at[core, pl.ds(where(me), rows)]
             theirs = full.at[core, pl.ds(where(o), rows)]
-            copy(mine, mine, send_sem.at[o], recv_sem.at[me], target(o)).wait_send()
             copy(theirs, theirs, send_sem.at[o], recv_sem.at[o], target(o)).wait_recv()
 
         loop3(me, body)
@@ -569,18 +595,77 @@
         rows = full.at[half, pl.ds(i * PART, PART)]
         return copy(rows, rows, gc_send.at[i], gc_recv.at[i], at(other_core))
 
+    def settle(where, me, target, send_sem, recv_sem, rows):
+        def body(j, o):
+            mine = full.at[core, pl.ds(where(me), rows)]
+            copy(mine, mine, send_sem.at[o], recv_sem.at[me], target(o)).wait_send()
+
+        loop3(me, body)
+
+    def store_params(i, half, slot):
+        rows = pl.ds(i * PART, PART)
+        return pltpu.make_async_copy(
+            full.at[half, rows], params_out.at[half, rows], load_sem.at[5 + slot]
+        )
+
     gather(*g1a)
     to_core(0, core).start()
     gather(*g1b)
     to_core(1, core).start()
+    store_mine = pltpu.make_async_copy(full.at[core], params_out.at[core], load_sem.at[5])
+    store_mine.start()
+
+    for k in range(8):
+        far_copy(k).wait_send()
+        near_copy(k, True).wait_send()
+    for args in ((act3, act_halo, ah_send, ah_recv), (cg3, cg_halo, ch_send, ch_recv)):
+        for c in halo_copies(*args):
+            c.wait_send()
+    drain(stat_a, 8, low, low_of, sa_send, sa_recv)
+    drain(stat_b, 16, high, high_of, sb_send, sb_recv)
+    drain(back_a, 8, low, low_of, ba_send, ba_recv)
+    drain(back_b, 16, high, high_of, bb_send, bb_recv)
+    clip_copy.wait_send()
+    for i in range(4):
+        core_copy(i).wait_send()
+    for which in range(2):
+        loop3((x, y)[which], lambda j, o: s1_copy(which, (x, y)[which], o, o).wait_send())
+        loop3((y, x)[which], lambda j, o: s2_copy(which, (y, x)[which], o).wait_send())
+
+    def s3_sent(j, _):
+        s3_copy(lax.rem(z + j, 8), z).wait_send()
+        return 0
+
+    lax.fori_loop(1, 8, s3_sent, 0)
+    for args in (g3, g2a, g2b, g1a, g1b):
+        settle(*args)
+
+    for i in range(2):
+        to_core(i, 1 - core).wait_recv()
+        store_params(i, 1 - core, 1 + i).start()
     for i in range(2):
         to_core(i, core).wait_send()
-        to_core(i, 1 - core).wait_recv()
-    params_out[...] = full[...]
-
-    for k in range(8):
-        far_copy(k).wait_send()
-        near_copy(k).wait_send()
+    store_grad.wait()
+    store_mine.wait()
+    for i in range(2):
+        store_params(i, 1 - core, 1 + i).wait()
+
+
+def finish_kernel(grad, params, gain, bias, grad_out, spatial, temporal, gain_out, bias_out):
+    step = pl.program_id(0)
+    grad_out[...] = grad[...]
+
+    @pl.when(step < 3)
+    def put_spatial():
+        for half in range(2):
+            spatial[:, :, half * 128 : (half + 1) * 128] = params[half].astype(F32)
+
+    @pl.when(step == 3)
+    def put_temporal():
+        for half in range(2):
+            temporal[:, :, half * 128 : (half + 1) * 128] = params[half].astype(F32)
+        gain_out[...] = gain[0]
+        bias_out[...] = bias[0]
 
 
 def local(block_input, cotangent, group_norm_gain, group_norm_bias, w_spatial, w_temporal):
@@ -591,7 +676,6 @@
         pltpu.VMEM((PIXELS, CHANNELS), BF16),
         pltpu.VMEM((3, PIXELS, CHANNELS), BF16),
         pltpu.VMEM((PADDED, 3 * CHANNELS), BF16),
-        pltpu.VMEM((3, 3 * CHANNELS, PIXELS), BF16),
         pltpu.VMEM((PADDED, 3 * CHANNELS), BF16),
         pltpu.VMEM((PIXELS, CHANNELS), BF16),
         pltpu.VMEM((CHANNELS, PIXELS), BF16),
@@ -618,7 +702,8 @@
         pltpu.VMEM((2 * SIXTEENTH, 128), F32),
         pltpu.VMEM((8, SHARD, 128), F32),
         pltpu.VMEM((2, HALF_ROWS, 128), BF16),
-        dma((4,)),
+        pltpu.VMEM((PIXELS, CHANNELS), BF16),
+        dma((8,)),
         dma((8,)), dma((8,)), dma((8,)), dma((8,)),
         dma((2,)), dma((2,)), dma((2,)), dma((2,)),
         dma((8,)), dma((8,)), dma((16,)), dma((16,)),
@@ -639,7 +724,7 @@
             jax.ShapeDtypeStruct((1, CHANNELS), F32),
         ),
         in_specs=[any_space, any_space, vmem, vmem, any_space, any_space],
-        out_specs=(vmem, vmem, vmem, vmem),
+        out_specs=(any_space, any_space, vmem, vmem),
         scratch_shapes=scratch,
         compiler_params=pltpu.CompilerParams(
             collective_id=0, has_side_effects=True, vmem_limit_bytes=56 * 2**20
@@ -652,14 +737,41 @@
         w_spatial.reshape(9 * CHANNELS, CHANNELS),
         w_temporal,
     )
-    params = params.reshape(2, TAPS, CHANNELS, 128).transpose(1, 2, 0, 3)
-    params = params.reshape(TAPS, CHANNELS, CHANNELS).astype(F32)
+    params = params.reshape(2, TAPS, CHANNELS, 128)
+    whole = pl.BlockSpec((1, CHANNELS), lambda i: (0, 0))
+    line = pl.BlockSpec((CHANNELS,), lambda i: (0,))
+    block = pl.BlockSpec((BLOCK, CHANNELS), lambda i: (i, 0))
+    grad, spatial, temporal, gain_grad, bias_grad = pl.pallas_call(
+        finish_kernel,
+        grid=(4,),
+        out_shape=(
+            jax.ShapeDtypeStruct((PIXELS, CHANNELS), BF16),
+            jax.ShapeDtypeStruct((9, CHANNELS, CHANNELS), F32),
+            jax.ShapeDtypeStruct((3, CHANNELS, CHANNELS), F32),
+            jax.ShapeDtypeStruct((CHANNELS,), F32),
+            jax.ShapeDtypeStruct((CHANNELS,), F32),
+        ),
+        in_specs=[
+            block,
+            pl.BlockSpec((2, 3, CHANNELS, 128), lambda i: (0, i, 0, 0)),
+            whole,
+            whole,
+        ],
+        out_specs=(
+            block,
+            pl.BlockSpec((3, CHANNELS, CHANNELS), lambda i: (jnp.minimum(i, 2), 0, 0)),
+            pl.BlockSpec((3, CHANNELS, CHANNELS), lambda i: (0, 0, 0)),
+            line,
+            line,
+        ),
+        compiler_params=pltpu.CompilerParams(vmem_limit_bytes=32 * 2**20),
+    )(grad, params, gain_grad, bias_grad)
     return (
         grad.reshape(1, ROWS_DEV, COLS, CHANNELS),
-        params[:9],
-        params[9:],
-        gain_grad.reshape(CHANNELS),
-        bias_grad.reshape(CHANNELS),
+        spatial,
+        temporal,
+        gain_grad,
+        bias_grad,
     )
 
 

time: 124 us -> 124 us (level)
  Pallas kernels: 117 us -> 119 us
  other arithmetic: 1.74 us -> 0 us
    pallas_call x0 -> x1, Pallas kernels: none -> 2.67 us  [local(): pl.pallas_call(finish_kernel, grid=(4,), out_shape=(jax.ShapeDtypeStruct(...]
    slice x2 -> x0, local copies, waits for them, and re-layouts: 2.56 us -> none  [the longest x1 1.61 us: local(): params[:9]]
    unnamed x9 -> x8, local copies, waits for them, and re-layouts: 1.97 us -> 3.75 us
    convert_element_type x1 -> x0, other arithmetic: 1.74 us -> none  [local(): params = params.reshape(TAPS, CHANNELS, CHANNELS).astype(F32)]
where the time goes in v2:
time: 124 us
  Pallas kernels  119 us (96%)
  local copies, waits for them, and re-layouts  3.75 us (3%)
    pallas_call x1, Pallas kernels, local(): pl.pallas_call(kernel, out_shape=(jax.ShapeDtypeStruct((PIXELS, CHANNELS)...  117 us
    unnamed x8, local copies, waits for them, and re-layouts  3.75 us
    pallas_call x1, Pallas kernels, local(): pl.pallas_call(finish_kernel, grid=(4,), out_shape=(jax.ShapeDtypeStruct(...  2.67 us

profile of v2, /device:TPU:1, one launch (start us, length us, event | category | flops | bytes accessed | tf_op | source)
XLA Modules:
  0.0 123.7 jit_solution(12492693798884088014)
XLA Ops:
  0.6 116.6 %shard_map.101 = (bf16[1280,256]{1,0:T(8,128)(2,1)}, bf16[2,3072,128]{2,1,0:T(8,128)(2,1)}, f32[1,256]{1,0:T(1,128)}, f32[1,256]{1,0:T(1,128)}) custom-call(bf16[1280,256]{1,0:T(8,128)(2,1)} %bitcast.9, bf16[1280,256]{1,0:T(8,128)(2,1)} %bitcast.10, f32[1,256]{1,0:T(1,128)} %bitcast.11, f32[1,256]{1,0:T(1,128)} %bitcast.12, bf16[2304,256]{1,0:T(8,128)(2,1)} %bitcast.8, ...), custom_call_target="tpu_custom_call" | custom-call | tf_op jit(solution)/shard_map/pallas_call | solution.py:718
  117.3 0.0 copy-start
  117.3 1.4 %copy-done = bf16[2,3072,128]{2,1,0:T(8,128)(2,1)S(1)} copy-done((bf16[2,3072,128]{2,1,0:T(8,128)(2,1)S(1)}, bf16[2,3072,128]{2,1,0:T(8,128)(2,1)}, u32[]{:S(2)}) %copy-start) | copy-done | bytes 1572888
  118.7 0.0 copy-start.1
  118.7 1.1 copy-done.1
  119.8 0.0 copy-start.2
  119.8 0.6 copy-done.2
  120.4 0.0 copy-start.3
  120.4 0.6 copy-done.3
  121.0 2.7 %shard_map.102 = (bf16[1280,256]{1,0:T(8,128)(2,1)}, f32[9,256,256]{2,1,0:T(8,128)}, f32[3,256,256]{2,1,0:T(8,128)}, f32[256]{0:T(256)}, f32[256]{0:T(256)}) custom-call(bf16[1280,256]{1,0:T(8,128)(2,1)S(1)} %copy-done.1, bf16[2,12,256,128]{3,2,1,0:T(8,128)(2,1)S(1)} %bitcast.7, f32[1,256]{1,0:T(1,128)S(1)} %copy-done.2, f32[1,256]{1,0:T(1,128)S(1)} %copy-done.3), custom_call_target="tpu_custom_call" | custom-call | tf_op jit(solution)/shard_map/pallas_call | solution.py:744
Async XLA Ops:
  117.3 1.4 %copy-start = (bf16[2,3072,128]{2,1,0:T(8,128)(2,1)S(1)}, bf16[2,3072,128]{2,1,0:T(8,128)(2,1)}, u32[]{:S(2)}) copy-start(bf16[2,3072,128]{2,1,0:T(8,128)(2,1)} %get-tuple-element.15) | copy-start | bytes 4718596
  118.7 1.1 copy-start.1
  119.8 0.6 copy-start.2
  120.4 0.6 copy-start.3

commit v3 on v2

--- a/solution.py
+++ b/solution.py
@@ -39,8 +39,8 @@
     grad_out, params_out, gain_out, bias_out,
     xv, cots, act3, cg3, conv, convt, wsp, wspt, wt, wtt, pre_grad,
     act_halo, cg_halo, stat_a, stat_b, back_a, back_b, clip_sums,
-    part, core_in, in1a, in1b, mid_a, mid_b, in2a, in2b, mid2, in3, full, grad_v,
-    load_sem, far_send, far_recv, near_send, near_recv,
+    part, core_in, in1a, in1b, mid_a, mid_b, in2a, in2b, mid2, in3, full, grad_v, passing,
+    load_sem, far_send, far_recv, near_send, near_recv, leg_send, leg_recv,
     ah_send, ah_recv, ch_send, ch_recv,
     sa_send, sa_recv, sb_send, sb_recv, ba_send, ba_recv, bb_send, bb_recv, clip_sem,
     core_send, core_recv, s1_send, s1_recv, s2_send, s2_recv, s3_send, s3_recv,
@@ -114,12 +114,25 @@
         greet((1 - clip, seq + 8 * (j - zh)))
         return 0
 
-    lax.fori_loop(1, 8, greet_low, 0)
+    z_up = lax.rem(z + 3, 8)
+    z_down = lax.rem(z + 5, 8)
+
+    def wrapped(source_z):
+        return 1 - jnp.minimum(source_z // 2, 1)
+
+    def at_zy(zz, yy):
+        return (lax.rem(zz, 2), seq + 8 * (zz // 2 - zh) + 32 * (yy - y))
+
+    leg1_to = at_zy(z_up, y)
+    leg2_to = at_zy(z_up, lax.rem(y + 4 - wrapped(z_down), 4))
+    leg2_from = at_zy(z_down, lax.rem(y + wrapped(lax.rem(z + 2, 8)), 4))
+
     lax.fori_loop(1, 16, greet_high, 0)
     lax.fori_loop(0, 4, greet_z, 0)
+    greet(leg2_from)
     greet(at(up))
     greet(at(down))
-    pl.semaphore_wait(barrier, 7 + 15 + 4 + 2)
+    lax.fori_loop(1, 8, greet_low, 0)
 
     def far_copy(k):
         rows = pl.ds(ORDER[k] * COLS, COLS)
@@ -134,13 +147,13 @@
             near_send.at[k], near_recv.at[k], at(near_to),
         )
 
-    for k in range(8):
-        far_copy(k).start()
-
-    @pl.when(x_high == 1)
-    def send_own():
-        for k in range(8):
-            near_copy(k, True).start()
+    detour_rows = pl.ds(ORDER[7] * COLS, COLS)
+
+    def leg1_copy():
+        return copy(g_hbm.at[detour_rows], passing, leg_send.at[0], leg_recv, leg1_to)
+
+    def leg2_copy():
+        return copy(passing, cots.at[2, detour_rows], leg_send.at[1], far_recv.at[7], leg2_to)
 
     def exchange(buf, n, me, target, send_sem, recv_sem):
         def body(j, _):
@@ -205,7 +218,16 @@
     zero8 = jnp.zeros((8, CHANNELS), F32)
     a, b = lax.fori_loop(0, ROWS_DEV, stat_body, (zero8, zero8))
     stat_a[low] = pack_rows(jnp.sum(a, axis=0, keepdims=True), jnp.sum(b, axis=0, keepdims=True))
+    pl.semaphore_wait(barrier, 15 + 4 + 1 + 2 + 7)
+
     exchange(stat_a, 8, low, low_of, sa_send, sa_recv)
+    leg1_copy().start()
+    far_copy(0).start()
+
+    @pl.when(x_high == 1)
+    def send_own():
+        for k in range(8):
+            near_copy(k, True).start()
 
     load_wt.wait()
     load_wsp.wait()
@@ -220,6 +242,8 @@
 
     stat_b[high] = collect(stat_a, 8, low, low_of, sa_send, sa_recv)
     exchange(stat_b, 16, high, high_of, sb_send, sb_recv)
+    for k in (1, 2, 3):
+        far_copy(k).start()
     load_g.wait()
     moments = group_sum(collect(stat_b, 16, high, high_of, sb_send, sb_recv)) * (1.0 / COUNT)
     mean = moments[0:1]
@@ -280,15 +304,16 @@
     act_row(0)
     act_row(ROWS_DEV - 1)
     send_halo(act3, act_halo, ah_send, ah_recv)
+    leg1_copy().wait_recv()
+    leg2_copy().start()
+    far_copy(4).start()
+    far_copy(5).start()
 
     def act_body(r, _):
         act_row(r)
         return 0
 
     lax.fori_loop(1, ROWS_DEV - 1, act_body, 0)
-    forward(0)
-    take_halo(act3, act_halo, ah_send, ah_recv)
-    forward(1)
 
     def convolve(buf, weights, i):
         total = None
@@ -301,20 +326,6 @@
             total = term if total is None else total + term
         return total
 
-    def conv_body(i, _):
-        conv[pl.ds(i * BLOCK, BLOCK), :] = convolve(act3, wsp, i).astype(BF16)
-        return 0
-
-    lax.fori_loop(0, PIXELS // BLOCK, conv_body, 0)
-    forward(2)
-
-    def turn_conv(i, _):
-        src = pl.ds(pl.multiple_of(i * 128, 128), 128)
-        convt[:, src] = conv[src, :].T
-        return 0
-
-    lax.fori_loop(0, PIXELS // 128, turn_conv, 0)
-
     keep1 = jnp.where(frame < FRAMES - 1, 1.0, 0.0).astype(F32)
     keep2 = jnp.where(frame < FRAMES - 2, 1.0, 0.0).astype(F32)
 
@@ -360,23 +371,41 @@
             at(other_core),
         )
 
-    forward(3)
+    forward(0)
+    forward(1)
     cg_row(0)
     cg_row(1)
     send_halo(cg3, cg_halo, ch_send, ch_recv)
+    far_copy(6).start()
+    forward(2)
+    take_halo(act3, act_halo, ah_send, ah_recv)
+
+    def conv_body(i, _):
+        conv[pl.ds(i * BLOCK, BLOCK), :] = convolve(act3, wsp, i).astype(BF16)
+        return 0
+
+    lax.fori_loop(0, PIXELS // BLOCK, conv_body, 0)
+    forward(3)
+
+    def turn_conv(i, _):
+        src = pl.ds(pl.multiple_of(i * 128, 128), 128)
+        convt[:, src] = conv[src, :].T
+        return 0
+
+    lax.fori_loop(0, PIXELS // 128, turn_conv, 0)
+    cg_row(2)
     forward(4)
-    cg_row(2)
+    cg_row(3)
     forward(5)
-    cg_row(3)
-    forward(6)
     cg_row(4)
     temporal_half(0)
-    forward(7)
     for dy in range(3):
         spatial_half(0, dy)
+    forward(6)
     cg_row(5)
+    forward(7)
+    cg_row(6)
     take_halo(cg3, cg_halo, ch_send, ch_recv)
-    cg_row(6)
     cg_row(7)
     temporal_half(1)
     core_copy(3).start()
@@ -616,8 +645,11 @@
     store_mine.start()
 
     for k in range(8):
+        near_copy(k, True).wait_send()
+    for k in range(7):
         far_copy(k).wait_send()
-        near_copy(k, True).wait_send()
+    leg1_copy().wait_send()
+    leg2_copy().wait_send()
     for args in ((act3, act_halo, ah_send, ah_recv), (cg3, cg_halo, ch_send, ch_recv)):
         for c in halo_copies(*args):
             c.wait_send()
@@ -703,8 +735,9 @@
         pltpu.VMEM((8, SHARD, 128), F32),
         pltpu.VMEM((2, HALF_ROWS, 128), BF16),
         pltpu.VMEM((PIXELS, CHANNELS), BF16),
+        pltpu.VMEM((COLS, CHANNELS), BF16),
         dma((8,)),
-        dma((8,)), dma((8,)), dma((8,)), dma((8,)),
+        dma((8,)), dma((8,)), dma((8,)), dma((8,)), dma((2,)), dma,
         dma((2,)), dma((2,)), dma((2,)), dma((2,)),
         dma((8,)), dma((8,)), dma((16,)), dma((16,)),
         dma((8,)), dma((8,)), dma((16,)), dma((16,)),
@@ -764,7 +797,7 @@
             line,
             line,
         ),
-        compiler_params=pltpu.CompilerParams(vmem_limit_bytes=32 * 2**20),
+        compiler_params=pltpu.CompilerParams(vmem_limit_bytes=60 * 2**20),
     )(grad, params, gain_grad, bias_grad)
     return (
         grad.reshape(1, ROWS_DEV, COLS, CHANNELS),

time: 124 us -> 107 us (0.86)
  Pallas kernels: 119 us -> 106 us
  local copies, waits for them, and re-layouts: 3.75 us -> 0 us
    pallas_call x1, Pallas kernels: 117 us -> 102 us  [local(): pl.pallas_call(kernel, out_shape=(jax.ShapeDtypeStruct((PIXELS, CHANNELS)...]
    unnamed x8 -> x0, local copies, waits for them, and re-layouts: 3.75 us -> none
    pallas_call x1, Pallas kernels: 2.67 us -> 4.48 us  [local(): pl.pallas_call(finish_kernel, grid=(4,), out_shape=(jax.ShapeDtypeStruct(...]
where the time goes in v3:
time: 107 us
  Pallas kernels  106 us (99%)
    pallas_call x1, Pallas kernels, local(): pl.pallas_call(kernel, out_shape=(jax.ShapeDtypeStruct((PIXELS, CHANNELS)...  102 us
    pallas_call x1, Pallas kernels, local(): pl.pallas_call(finish_kernel, grid=(4,), out_shape=(jax.ShapeDtypeStruct(...  4.48 us

profile of v3, /device:TPU:1, one launch (start us, length us, event | category | flops | bytes accessed | tf_op | source)
XLA Modules:
  0.0 107.0 jit_solution(4067886098762999753)
XLA Ops:
  0.6 101.8 %shard_map.101 = (bf16[1280,256]{1,0:T(8,128)(2,1)}, bf16[2,3072,128]{2,1,0:T(8,128)(2,1)}, f32[1,256]{1,0:T(1,128)}, f32[1,256]{1,0:T(1,128)}) custom-call(bf16[1280,256]{1,0:T(8,128)(2,1)} %bitcast.9, bf16[1280,256]{1,0:T(8,128)(2,1)} %bitcast.10, f32[1,256]{1,0:T(1,128)} %bitcast.11, f32[1,256]{1,0:T(1,128)} %bitcast.12, bf16[2304,256]{1,0:T(8,128)(2,1)} %bitcast.8, ...), custom_call_target="tpu_custom_call" | custom-call | tf_op jit(solution)/shard_map/pallas_call | solution.py:751
  102.5 4.5 %shard_map.102 = (bf16[1280,256]{1,0:T(8,128)(2,1)}, f32[9,256,256]{2,1,0:T(8,128)}, f32[3,256,256]{2,1,0:T(8,128)}, f32[256]{0:T(256)}, f32[256]{0:T(256)}) custom-call(bf16[1280,256]{1,0:T(8,128)(2,1)} %get-tuple-element.14.grad, bf16[2,12,256,128]{3,2,1,0:T(8,128)(2,1)} %bitcast.7, f32[1,256]{1,0:T(1,128)} %get-tuple-element.16.gain, ...), custom_call_target="tpu_custom_call" | custom-call | tf_op jit(solution)/shard_map/pallas_call | solution.py:777

commit v4 on v3

--- a/solution.py
+++ b/solution.py
@@ -28,10 +28,11 @@
 
 TAPS = 12
 HALF_ROWS = TAPS * CHANNELS
-PART = HALF_ROWS // 2
+PARTS = 4
+PART = HALF_ROWS // PARTS
 QUARTER = PART // 4
-SIXTEENTH = PART // 16
-SHARD = 2 * SIXTEENTH // 4
+SHARD = QUARTER // 4
+PART_ORDER = (3, 0, 2, 1)
 
 
 def kernel(
@@ -39,8 +40,8 @@
     grad_out, params_out, gain_out, bias_out,
     xv, cots, act3, cg3, conv, convt, wsp, wspt, wt, wtt, pre_grad,
     act_halo, cg_halo, stat_a, stat_b, back_a, back_b, clip_sums,
-    part, core_in, in1a, in1b, mid_a, mid_b, in2a, in2b, mid2, in3, full, grad_v, passing,
-    load_sem, far_send, far_recv, near_send, near_recv, leg_send, leg_recv,
+    part, core_in, in1, mid, in2, mid2, in3, full, grad_v, passing,
+    load_sem, store_sem, far_send, far_recv, near_send, near_recv, leg1_send, leg1_recv, leg2_send,
     ah_send, ah_recv, ch_send, ch_recv,
     sa_send, sa_recv, sb_send, sb_recv, ba_send, ba_recv, bb_send, bb_recv, clip_sem,
     core_send, core_recv, s1_send, s1_recv, s2_send, s2_recv, s3_send, s3_recv,
@@ -147,13 +148,19 @@
             near_send.at[k], near_recv.at[k], at(near_to),
         )
 
-    detour_rows = pl.ds(ORDER[7] * COLS, COLS)
-
-    def leg1_copy():
-        return copy(g_hbm.at[detour_rows], passing, leg_send.at[0], leg_recv, leg1_to)
-
-    def leg2_copy():
-        return copy(passing, cots.at[2, detour_rows], leg_send.at[1], far_recv.at[7], leg2_to)
+    def leg1_copy(i):
+        rows = pl.ds(ORDER[6 + i] * COLS, COLS)
+        return copy(g_hbm.at[rows], passing.at[i], leg1_send.at[i], leg1_recv.at[i], leg1_to)
+
+    def leg2_copy(i):
+        rows = pl.ds(ORDER[6 + i] * COLS, COLS)
+        return copy(
+            passing.at[i], cots.at[2, rows], leg2_send.at[i], far_recv.at[6 + i], leg2_to
+        )
+
+    def pass_detour(i):
+        leg1_copy(i).wait_recv()
+        leg2_copy(i).start()
 
     def exchange(buf, n, me, target, send_sem, recv_sem):
         def body(j, _):
@@ -221,8 +228,9 @@
     pl.semaphore_wait(barrier, 15 + 4 + 1 + 2 + 7)
 
     exchange(stat_a, 8, low, low_of, sa_send, sa_recv)
-    leg1_copy().start()
+    leg1_copy(0).start()
     far_copy(0).start()
+    leg1_copy(1).start()
 
     @pl.when(x_high == 1)
     def send_own():
@@ -304,10 +312,9 @@
     act_row(0)
     act_row(ROWS_DEV - 1)
     send_halo(act3, act_halo, ah_send, ah_recv)
-    leg1_copy().wait_recv()
-    leg2_copy().start()
     far_copy(4).start()
     far_copy(5).start()
+    pass_detour(0)
 
     def act_body(r, _):
         act_row(r)
@@ -362,7 +369,7 @@
         )
         put(dy * chunk_rows, v, h > 0)
 
-    chunk_rows = 3 * CHANNELS
+    chunk_rows = PART
 
     def core_copy(i):
         rows = pl.ds(i * chunk_rows, chunk_rows)
@@ -372,11 +379,11 @@
         )
 
     forward(0)
+    pass_detour(1)
     forward(1)
     cg_row(0)
     cg_row(1)
     send_halo(cg3, cg_halo, ch_send, ch_recv)
-    far_copy(6).start()
     forward(2)
     take_halo(act3, act_halo, ah_send, ah_recv)
 
@@ -409,7 +416,7 @@
     cg_row(7)
     temporal_half(1)
     core_copy(3).start()
-    for dy in (0, 1, 2):
+    for dy in PART_ORDER[1:]:
         spatial_half(1, dy)
         core_copy(dy).start()
 
@@ -423,89 +430,87 @@
         b = b + jnp.sum((v * xhat).reshape(BLOCK // 8, 8, CHANNELS), axis=0)
         return a, b
 
-    def s1_copy(which, me, o, peer):
-        buf = (in1a, in1b)[which]
-        target = (at_x, at_y)[which]
+    def first_axis(p):
+        return ((x, at_x), (y, at_y))[p // 2]
+
+    def second_axis(p):
+        return ((y, at_y), (x, at_x))[p // 2]
+
+    def loop3(me, body):
+        def step(j, _):
+            body(lax.rem(me + j, 4))
+            return 0
+
+        lax.fori_loop(1, 4, step, 0)
+
+    def s1_copy(p, o):
+        me, target = first_axis(p)
         return copy(
-            part.at[core, pl.ds(which * PART + o * QUARTER, QUARTER)], buf.at[me],
-            s1_send.at[which, o], s1_recv.at[which, me], target(peer),
-        )
-
-    def add_core(i):
-        core_copy(i).wait_recv()
-        rows = pl.ds(i * chunk_rows, chunk_rows)
+            part.at[core, pl.ds(p * PART + o * QUARTER, QUARTER)], in1.at[p, me],
+            s1_send.at[p, o], s1_recv.at[p, me], target(o),
+        )
+
+    def s1_arrived(p, o):
+        _, target = first_axis(p)
+        return copy(in1.at[p, o], in1.at[p, o], s1_send.at[p, o], s1_recv.at[p, o], target(o))
+
+    def s2_copy(p, o):
+        me, target = second_axis(p)
+        return copy(
+            mid.at[p, pl.ds(o * SHARD, SHARD)], in2.at[p, me],
+            s2_send.at[p, o], s2_recv.at[p, me], target(o),
+        )
+
+    def s2_arrived(p, o):
+        _, target = second_axis(p)
+        return copy(in2.at[p, o], in2.at[p, o], s2_send.at[p, o], s2_recv.at[p, o], target(o))
+
+    def add_core(p):
+        core_copy(p).wait_recv()
+        rows = pl.ds(p * PART, PART)
         part[core, rows, :] = part[core, rows, :] + core_in[rows, :]
-        which = i // 2
-        me = (x, y)[which]
-        for o in (2 * (i % 2), 2 * (i % 2) + 1):
-            @pl.when(me != o)
-            def send_slice():
-                s1_copy(which, me, o, o).start()
+        loop3(first_axis(p)[0], lambda o: s1_copy(p, o).start())
 
     sums = (zero8, zero8)
-    for i, chunk in enumerate((3, 0, 1, 2)):
+    for i, p in enumerate(PART_ORDER):
         sums = back_block(i, sums)
-        add_core(chunk)
+        add_core(p)
     a, b = sums
     back_a[low] = pack_rows(jnp.sum(a, axis=0, keepdims=True), jnp.sum(b, axis=0, keepdims=True))
     exchange(back_a, 8, low, low_of, ba_send, ba_recv)
 
-    def loop3(me, body):
-        def step(j, _):
-            body(j, lax.rem(me + j, 4))
-            return 0
-
-        lax.fori_loop(1, 4, step, 0)
+    def s1_finish(p):
+        me, _ = first_axis(p)
+        loop3(me, lambda o: s1_arrived(p, o).wait_recv())
+        total = part[core, pl.ds(p * PART + me * QUARTER, QUARTER), :]
+        for j in range(1, 4):
+            total = total + in1[p, lax.rem(me + j, 4)]
+        mid[p] = total
+        loop3(second_axis(p)[0], lambda o: s2_copy(p, o).start())
+
+    def s3_copy(o, slot):
+        return copy(mid2.at[o // 2], in3.at[slot], s3_send.at[o], s3_recv.at[slot], at_z(o))
+
+    def s2_finish(p):
+        me, _ = second_axis(p)
+        loop3(me, lambda o: s2_arrived(p, o).wait_recv())
+        total = mid[p, pl.ds(me * SHARD, SHARD), :]
+        for j in range(1, 4):
+            total = total + in2[p, lax.rem(me + j, 4)]
+        mid2[p] = total
+        for o in (2 * p, 2 * p + 1):
+            @pl.when(z != o)
+            def send_shard():
+                s3_copy(o, z).start()
+
+    for p in PART_ORDER:
+        s1_finish(p)
 
     back_b[high] = collect(back_a, 8, low, low_of, ba_send, ba_recv)
     exchange(back_b, 16, high, high_of, bb_send, bb_recv)
 
-    def s1_finish(which):
-        me = (x, y)[which]
-        buf = (in1a, in1b)[which]
-        mid = (mid_a, mid_b)[which]
-
-        def wait(j, o):
-            s1_copy(which, o, o, o).wait_recv()
-
-        loop3(me, wait)
-        mine = pl.ds(which * PART + me * QUARTER, QUARTER)
-        total = part[core, mine, :]
-        for j in range(1, 4):
-            total = total + buf[lax.rem(me + j, 4)]
-        mid[...] = total
-
-    def s2_copy(which, me, o):
-        mid = (mid_a, mid_b)[which]
-        buf = (in2a, in2b)[which]
-        target = (at_y, at_x)[which]
-        return copy(
-            mid.at[pl.ds(o * SIXTEENTH, SIXTEENTH)], buf.at[me],
-            s2_send.at[which, o], s2_recv.at[which, me], target(o),
-        )
-
-    def s2_start(which):
-        me = (y, x)[which]
-        loop3(me, lambda j, o: s2_copy(which, me, o).start())
-
-    def s2_finish(which):
-        me = (y, x)[which]
-        mid = (mid_a, mid_b)[which]
-        buf = (in2a, in2b)[which]
-
-        def wait(j, o):
-            s2_copy(which, o, o).wait_recv()
-
-        loop3(me, wait)
-        total = mid[pl.ds(me * SIXTEENTH, SIXTEENTH), :]
-        for j in range(1, 4):
-            total = total + buf[lax.rem(me + j, 4)]
-        mid2[which * SIXTEENTH : (which + 1) * SIXTEENTH, :] = total
-
-    s1_finish(1)
-    s2_start(1)
-    s1_finish(0)
-    s2_start(0)
+    for p in PART_ORDER:
+        s2_finish(p)
 
     sums = collect(back_b, 16, high, high_of, bb_send, bb_recv)
     clip_sums[clip] = sums
@@ -525,37 +530,64 @@
         return 0
 
     lax.fori_loop(0, ROWS_DEV, out_body, 0)
-    store_grad = pltpu.make_async_copy(grad_v, grad_out, load_sem.at[4])
+    store_grad = pltpu.make_async_copy(grad_v, grad_out, store_sem.at[0])
     store_grad.start()
 
-    def s3_copy(o, slot):
-        return copy(
-            mid2.at[pl.ds(SHARD * (o // 2), SHARD)], in3.at[slot],
-            s3_send.at[o], s3_recv.at[slot], at_z(o),
-        )
-
-    def s3_start(which):
-        def body(j, _):
-            o = 4 * which + j
-
-            @pl.when(o != z)
-            def send_shard():
-                s3_copy(o, z).start()
-
-            return 0
-
-        lax.fori_loop(0, 4, body, 0)
-
-    def s3_wait(j, _):
-        o = lax.rem(z + j, 8)
-        s3_copy(o, o).wait_recv()
-        return 0
-
-    s2_finish(1)
-    s3_start(1)
-    s2_finish(0)
-    s3_start(0)
-    in3[z] = mid2[pl.ds(SHARD * zh, SHARD), :]
+    def quarter_at(p, first):
+        return pl.multiple_of(p * PART + QUARTER * first, QUARTER)
+
+    def shard_at(p, first, second):
+        return pl.multiple_of(p * PART + QUARTER * first + SHARD * second, SHARD)
+
+    def own_shard(p):
+        return full.at[core, pl.ds(shard_at(p, first_axis(p)[0], second_axis(p)[0]), SHARD)]
+
+    def g3_copy(p, o):
+        rows = own_shard(p)
+        return copy(rows, rows, g3_send.at[o], g3_recv.at[p], at_zh(o))
+
+    def g2_copy(p, o, sender):
+        rows = full.at[core, pl.ds(shard_at(p, first_axis(p)[0], sender), SHARD)]
+        return copy(rows, rows, g2_send.at[p, o], g2_recv.at[p, sender], second_axis(p)[1](o))
+
+    def g1_copy(p, o, sender):
+        rows = full.at[core, pl.ds(quarter_at(p, sender), QUARTER)]
+        return copy(rows, rows, g1_send.at[p, o], g1_recv.at[p, sender], first_axis(p)[1](o))
+
+    def to_core(p, half):
+        rows = full.at[half, pl.ds(p * PART, PART)]
+        return copy(rows, rows, gc_send.at[p], gc_recv.at[p], at(other_core))
+
+    def store_params(p, half, slot):
+        rows = pl.ds(p * PART, PART)
+        return pltpu.make_async_copy(
+            full.at[half, rows], params_out.at[half, rows], store_sem.at[1 + slot * PARTS + p]
+        )
+
+    for p in PART_ORDER:
+        @pl.when(zh == p)
+        def finish_part():
+            in3[z] = mid2[p]
+
+            def arrived(j, _):
+                o = lax.rem(z + j, 8)
+                copy(in3.at[o], in3.at[o], s3_send.at[o], s3_recv.at[o], at_z(o)).wait_recv()
+                return 0
+
+            lax.fori_loop(1, 8, arrived, 0)
+            total = in3[0]
+            for o in range(1, 8):
+                total = total + in3[o]
+            where = pl.ds(shard_at(p, first_axis(p)[0], second_axis(p)[0]), SHARD)
+            full[core, where, :] = (total * SCALE).astype(BF16)
+            loop3(zh, lambda o: g3_copy(p, o).start())
+
+        @pl.when(zh != p)
+        def take_part():
+            g3_copy(p, zh + 1 - 2 * lax.rem(zh, 2)).wait_recv()
+
+        me, _ = second_axis(p)
+        loop3(me, lambda o: g2_copy(p, o, me).start())
 
     copy(
         clip_sums.at[1 - clip], clip_sums.at[1 - clip], clip_sem.at[0], clip_sem.at[1],
@@ -565,91 +597,23 @@
     bias_out[...] = both[0:1]
     gain_out[...] = both[1:2]
 
-    lax.fori_loop(1, 8, s3_wait, 0)
-    total = in3[0]
-    for o in range(1, 8):
-        total = total + in3[o]
-
-    def shard_at(o):
-        second = o // 2
-        first = 1 - second
-        base = second * (PART + QUARTER * y + SIXTEENTH * x)
-        base = base + first * (QUARTER * x + SIXTEENTH * y)
-        return pl.multiple_of(base + SHARD * lax.rem(o, 2), SHARD)
-
-    full[core, pl.ds(shard_at(zh), SHARD), :] = (total * SCALE).astype(BF16)
-
-    def spread(where, me, target, send_sem, recv_sem, rows):
-        def body(j, o):
-            place_at = full.at[core, pl.ds(where(me), rows)]
-            copy(place_at, place_at, send_sem.at[o], recv_sem.at[me], target(o)).start()
-
-        loop3(me, body)
-
-    def gather(where, me, target, send_sem, recv_sem, rows):
-        def body(j, o):
-            theirs = full.at[core, pl.ds(where(o), rows)]
-            copy(theirs, theirs, send_sem.at[o], recv_sem.at[o], target(o)).wait_recv()
-
-        loop3(me, body)
-
-    g3 = (shard_at, zh, at_zh, g3_send, g3_recv, SHARD)
-    spread(*g3)
-    gather(*g3)
-
-    def sixteenth_a(o):
-        return pl.multiple_of(QUARTER * x + SIXTEENTH * o, SIXTEENTH)
-
-    def sixteenth_b(o):
-        return pl.multiple_of(PART + QUARTER * y + SIXTEENTH * o, SIXTEENTH)
-
-    def quarter_a(o):
-        return pl.multiple_of(QUARTER * o, QUARTER)
-
-    def quarter_b(o):
-        return pl.multiple_of(PART + QUARTER * o, QUARTER)
-
-    g2a = (sixteenth_a, y, at_y, g2_send.at[0], g2_recv.at[0], SIXTEENTH)
-    g2b = (sixteenth_b, x, at_x, g2_send.at[1], g2_recv.at[1], SIXTEENTH)
-    g1a = (quarter_a, x, at_x, g1_send.at[0], g1_recv.at[0], QUARTER)
-    g1b = (quarter_b, y, at_y, g1_send.at[1], g1_recv.at[1], QUARTER)
-    spread(*g2a)
-    spread(*g2b)
-    gather(*g2a)
-    spread(*g1a)
-    gather(*g2b)
-    spread(*g1b)
-
-    def to_core(i, half):
-        rows = full.at[half, pl.ds(i * PART, PART)]
-        return copy(rows, rows, gc_send.at[i], gc_recv.at[i], at(other_core))
-
-    def settle(where, me, target, send_sem, recv_sem, rows):
-        def body(j, o):
-            mine = full.at[core, pl.ds(where(me), rows)]
-            copy(mine, mine, send_sem.at[o], recv_sem.at[me], target(o)).wait_send()
-
-        loop3(me, body)
-
-    def store_params(i, half, slot):
-        rows = pl.ds(i * PART, PART)
-        return pltpu.make_async_copy(
-            full.at[half, rows], params_out.at[half, rows], load_sem.at[5 + slot]
-        )
-
-    gather(*g1a)
-    to_core(0, core).start()
-    gather(*g1b)
-    to_core(1, core).start()
-    store_mine = pltpu.make_async_copy(full.at[core], params_out.at[core], load_sem.at[5])
-    store_mine.start()
+    for p in PART_ORDER:
+        loop3(second_axis(p)[0], lambda o: g2_copy(p, o, o).wait_recv())
+        me, _ = first_axis(p)
+        loop3(me, lambda o: g1_copy(p, o, me).start())
+
+    for p in PART_ORDER:
+        loop3(first_axis(p)[0], lambda o: g1_copy(p, o, o).wait_recv())
+        to_core(p, core).start()
+        store_params(p, core, 0).start()
 
     for k in range(8):
         near_copy(k, True).wait_send()
-    for k in range(7):
+    for k in range(6):
         far_copy(k).wait_send()
-    leg1_copy().wait_send()
-    leg2_copy().wait_send()
+    for i in range(2):
+        leg1_copy(i).wait_send()
+        leg2_copy(i).wait_send()
     for args in ((act3, act_halo, ah_send, ah_recv), (cg3, cg_halo, ch_send, ch_recv)):
         for c in halo_copies(*args):
             c.wait_send()
@@ -658,46 +622,63 @@
     drain(back_a, 8, low, low_of, ba_send, ba_recv)
     drain(back_b, 16, high, high_of, bb_send, bb_recv)
     clip_copy.wait_send()
-    for i in range(4):
-        core_copy(i).wait_send()
-    for which in range(2):
-        loop3((x, y)[which], lambda j, o: s1_copy(which, (x, y)[which], o, o).wait_send())
-        loop3((y, x)[which], lambda j, o: s2_copy(which, (y, x)[which], o).wait_send())
 
     def s3_sent(j, _):
         s3_copy(lax.rem(z + j, 8), z).wait_send()
         return 0
 
     lax.fori_loop(1, 8, s3_sent, 0)
-    for args in (g3, g2a, g2b, g1a, g1b):
-        settle(*args)
-
-    for i in range(2):
-        to_core(i, 1 - core).wait_recv()
-        store_params(i, 1 - core, 1 + i).start()
-    for i in range(2):
-        to_core(i, core).wait_send()
+    for p in range(PARTS):
+        @pl.when(zh == p)
+        def sent_part():
+            loop3(zh, lambda o: g3_copy(p, o).wait_send())
+
+    for p in range(PARTS):
+        core_copy(p).wait_send()
+        loop3(first_axis(p)[0], lambda o: s1_copy(p, o).wait_send())
+        loop3(second_axis(p)[0], lambda o: s2_copy(p, o).wait_send())
+        loop3(second_axis(p)[0], lambda o: g2_copy(p, o, second_axis(p)[0]).wait_send())
+        loop3(first_axis(p)[0], lambda o: g1_copy(p, o, first_axis(p)[0]).wait_send())
+
+    for p in PART_ORDER:
+        to_core(p, 1 - core).wait_recv()
+        store_params(p, 1 - core, 1).start()
     store_grad.wait()
-    store_mine.wait()
-    for i in range(2):
-        store_params(i, 1 - core, 1 + i).wait()
-
-
-def finish_kernel(grad, params, gain, bias, grad_out, spatial, temporal, gain_out, bias_out):
-    step = pl.program_id(0)
-    grad_out[...] = grad[...]
-
-    @pl.when(step < 3)
-    def put_spatial():
+    for p in PART_ORDER:
+        to_core(p, core).wait_send()
+        store_params(p, core, 0).wait()
+        store_params(p, 1 - core, 1).wait()
+
+
+def finish_kernel(
+    grad, params, gain, bias, grad_out, spatial, temporal, gain_out, bias_out,
+    params_v, out_v, sem,
+):
+    move_grad = pltpu.make_async_copy(grad, grad_out, sem.at[0])
+
+    def load(i):
+        taps = pl.ds(3 * i, 3)
+        return pltpu.make_async_copy(params.at[:, taps], params_v.at[:, taps], sem.at[1 + i])
+
+    def store(i):
+        target = spatial.at[pl.ds(3 * i, 3)] if i < 3 else temporal
+        return pltpu.make_async_copy(out_v.at[pl.ds(3 * i, 3)], target, sem.at[5 + i])
+
+    for i in range(4):
+        load(i).start()
+    move_grad.start()
+    gain_out[...] = gain[0]
+    bias_out[...] = bias[0]
+    for i in range(4):
+        load(i).wait()
         for half in range(2):
-            spatial[:, :, half * 128 : (half + 1) * 128] = params[half].astype(F32)
-
-    @pl.when(step == 3)
-    def put_temporal():
-        for half in range(2):
-            temporal[:, :, half * 128 : (half + 1) * 128] = params[half].astype(F32)
-        gain_out[...] = gain[0]
-        bias_out[...] = bias[0]
+            out_v[3 * i : 3 * i + 3, :, half * 128 : (half + 1) * 128] = params_v[
+                half, 3 * i : 3 * i + 3
+            ].astype(F32)
+        store(i).start()
+    move_grad.wait()
+    for i in range(4):
+        store(i).wait()
 
 
 def local(block_input, cotangent, group_norm_gain, group_norm_bias, w_spatial, w_temporal):
@@ -725,28 +706,26 @@
         pltpu.VMEM((2, 8, CHANNELS), F32),
         pltpu.VMEM((2, HALF_ROWS, 128), F32),
         pltpu.VMEM((HALF_ROWS, 128), F32),
-        pltpu.VMEM((4, QUARTER, 128), F32),
-        pltpu.VMEM((4, QUARTER, 128), F32),
-        pltpu.VMEM((QUARTER, 128), F32),
-        pltpu.VMEM((QUARTER, 128), F32),
-        pltpu.VMEM((4, SIXTEENTH, 128), F32),
-        pltpu.VMEM((4, SIXTEENTH, 128), F32),
-        pltpu.VMEM((2 * SIXTEENTH, 128), F32),
+        pltpu.VMEM((PARTS, 4, QUARTER, 128), F32),
+        pltpu.VMEM((PARTS, QUARTER, 128), F32),
+        pltpu.VMEM((PARTS, 4, SHARD, 128), F32),
+        pltpu.VMEM((PARTS, SHARD, 128), F32),
         pltpu.VMEM((8, SHARD, 128), F32),
         pltpu.VMEM((2, HALF_ROWS, 128), BF16),
         pltpu.VMEM((PIXELS, CHANNELS), BF16),
-        pltpu.VMEM((COLS, CHANNELS), BF16),
-        dma((8,)),
-        dma((8,)), dma((8,)), dma((8,)), dma((8,)), dma((2,)), dma,
+        pltpu.VMEM((2, COLS, CHANNELS), BF16),
+        dma((4,)), dma((1 + 2 * PARTS,)),
+        dma((8,)), dma((8,)), dma((8,)), dma((8,)),
+        dma((2,)), dma((2,)), dma((2,)),
         dma((2,)), dma((2,)), dma((2,)), dma((2,)),
         dma((8,)), dma((8,)), dma((16,)), dma((16,)),
         dma((8,)), dma((8,)), dma((16,)), dma((16,)),
         dma((2,)),
         dma((4,)), dma((4,)),
-        dma((2, 4)), dma((2, 4)), dma((2, 4)), dma((2, 4)),
+        dma((4, 4)), dma((4, 4)), dma((4, 4)), dma((4, 4)),
         dma((8,)), dma((8,)),
-        dma((4,)), dma((4,)), dma((2, 4)), dma((2, 4)), dma((2, 4)), dma((2, 4)),
-        dma((2,)), dma((2,)),
+        dma((4,)), dma((4,)), dma((4, 4)), dma((4, 4)), dma((4, 4)), dma((4, 4)),
+        dma((4,)), dma((4,)),
     ]
     grad, params, gain_grad, bias_grad = pl.pallas_call(
         kernel,
@@ -771,12 +750,8 @@
         w_temporal,
     )
     params = params.reshape(2, TAPS, CHANNELS, 128)
-    whole = pl.BlockSpec((1, CHANNELS), lambda i: (0, 0))
-    line = pl.BlockSpec((CHANNELS,), lambda i: (0,))
-    block = pl.BlockSpec((BLOCK, CHANNELS), lambda i: (i, 0))
     grad, spatial, temporal, gain_grad, bias_grad = pl.pallas_call(
         finish_kernel,
-        grid=(4,),
         out_shape=(
             jax.ShapeDtypeStruct((PIXELS, CHANNELS), BF16),
             jax.ShapeDtypeStruct((9, CHANNELS, CHANNELS), F32),
@@ -784,19 +759,13 @@
             jax.ShapeDtypeStruct((CHANNELS,), F32),
             jax.ShapeDtypeStruct((CHANNELS,), F32),
         ),
-        in_specs=[
-            block,
-            pl.BlockSpec((2, 3, CHANNELS, 128), lambda i: (0, i, 0, 0)),
-            whole,
-            whole,
+        in_specs=[any_space, any_space, vmem, vmem],
+        out_specs=(any_space, any_space, any_space, vmem, vmem),
+        scratch_shapes=[
+            pltpu.VMEM((2, TAPS, CHANNELS, 128), BF16),
+            pltpu.VMEM((TAPS, CHANNELS, CHANNELS), F32),
+            dma((9,)),
         ],
-        out_specs=(
-            block,
-            pl.BlockSpec((3, CHANNELS, CHANNELS), lambda i: (jnp.minimum(i, 2), 0, 0)),
-            pl.BlockSpec((3, CHANNELS, CHANNELS), lambda i: (0, 0, 0)),
-            line,
-            line,
-        ),
         compiler_params=pltpu.CompilerParams(vmem_limit_bytes=60 * 2**20),
     )(grad, params, gain_grad, bias_grad)
     return (

time: 107 us -> 126 us (1.18)
  Pallas kernels: 106 us -> 126 us
    pallas_call x1, Pallas kernels: 4.48 us -> 22.3 us  [local(): pl.pallas_call(finish_kernel, out_shape=(jax.ShapeDtypeStruct((PIXELS, CH...]
    pallas_call x1, Pallas kernels: 102 us -> 103 us  [local(): pl.pallas_call(kernel, out_shape=(jax.ShapeDtypeStruct((PIXELS, CHANNELS)...]
where the time goes in v4:
time: 126 us
  Pallas kernels  126 us (100%)
    pallas_call x1, Pallas kernels, local(): pl.pallas_call(kernel, out_shape=(jax.ShapeDtypeStruct((PIXELS, CHANNELS)...  103 us
    pallas_call x1, Pallas kernels, local(): pl.pallas_call(finish_kernel, out_shape=(jax.ShapeDtypeStruct((PIXELS, CH...  22.3 us

profile of v4, /device:TPU:1, one launch (start us, length us, event | category | flops | bytes accessed | tf_op | source)
XLA Modules:
  0.0 126.3 jit_solution(4653248178429836925)
XLA Ops:
  0.6 103.4 %shard_map.101 = (bf16[1280,256]{1,0:T(8,128)(2,1)}, bf16[2,3072,128]{2,1,0:T(8,128)(2,1)}, f32[1,256]{1,0:T(1,128)}, f32[1,256]{1,0:T(1,128)}) custom-call(bf16[1280,256]{1,0:T(8,128)(2,1)} %bitcast.9, bf16[1280,256]{1,0:T(8,128)(2,1)} %bitcast.10, f32[1,256]{1,0:T(1,128)} %bitcast.11, f32[1,256]{1,0:T(1,128)} %bitcast.12, bf16[2304,256]{1,0:T(8,128)(2,1)} %bitcast.8, ...), custom_call_target="tpu_custom_call" | custom-call | tf_op jit(solution)/shard_map/pallas_call | solution.py:730
  104.0 22.3 %shard_map.102 = (bf16[1280,256]{1,0:T(8,128)(2,1)}, f32[9,256,256]{2,1,0:T(8,128)}, f32[3,256,256]{2,1,0:T(8,128)}, f32[256]{0:T(256)}, f32[256]{0:T(256)}) custom-call(bf16[1280,256]{1,0:T(8,128)(2,1)} %get-tuple-element.14.grad, bf16[2,12,256,128]{3,2,1,0:T(8,128)(2,1)} %bitcast.7, f32[1,256]{1,0:T(1,128)} %get-tuple-element.16.gain, ...), custom_call_target="tpu_custom_call" | custom-call | tf_op jit(solution)/shard_map/pallas_call | solution.py:753

commit v5 on v4

--- a/solution.py
+++ b/solution.py
@@ -36,11 +36,11 @@
 
 
 def kernel(
-    x_hbm, g_hbm, gain_ref, bias_ref, wsp_hbm, wt_hbm,
-    grad_out, params_out, gain_out, bias_out,
+    x_hbm, g_hbm, gain_hbm, bias_hbm, wsp_hbm, wt_hbm,
+    grad_out, params_out, sums_out,
     xv, cots, act3, cg3, conv, convt, wsp, wspt, wt, wtt, pre_grad,
     act_halo, cg_halo, stat_a, stat_b, back_a, back_b, clip_sums,
-    part, core_in, in1, mid, in2, mid2, in3, full, grad_v, passing,
+    part, core_in, in1, mid, in2, mid2, in3, full, grad_v, passing, affine, sums_v,
     load_sem, store_sem, far_send, far_recv, near_send, near_recv, leg1_send, leg1_recv, leg2_send,
     ah_send, ah_recv, ch_send, ch_recv,
     sa_send, sa_recv, sb_send, sb_recv, ba_send, ba_recv, bb_send, bb_recv, clip_sem,
@@ -97,6 +97,10 @@
     load_g.start()
     load_wsp.start()
     load_wt.start()
+    load_gain = pltpu.make_async_copy(gain_hbm, affine.at[0], load_sem.at[4])
+    load_bias = pltpu.make_async_copy(bias_hbm, affine.at[1], load_sem.at[5])
+    load_gain.start()
+    load_bias.start()
 
     barrier = pltpu.get_barrier_semaphore()
 
@@ -256,8 +260,10 @@
     moments = group_sum(collect(stat_b, 16, high, high_of, sb_send, sb_recv)) * (1.0 / COUNT)
     mean = moments[0:1]
     rstd = lax.rsqrt(moments[1:2] - mean * mean + EPS)
-    gain = gain_ref[...]
-    bias = bias_ref[...]
+    load_gain.wait()
+    load_bias.wait()
+    gain = affine[0]
+    bias = affine[1]
 
     def forward(k):
         far_copy(k).wait_recv()
@@ -403,6 +409,10 @@
     cg_row(2)
     forward(4)
     cg_row(3)
+    drain(stat_a, 8, low, low_of, sa_send, sa_recv)
+    drain(stat_b, 16, high, high_of, sb_send, sb_recv)
+    for c in halo_copies(act3, act_halo, ah_send, ah_recv):
+        c.wait_send()
     forward(5)
     cg_row(4)
     temporal_half(0)
@@ -503,14 +513,94 @@
             def send_shard():
                 s3_copy(o, z).start()
 
+    for k in range(8):
+        near_copy(k, True).wait_send()
+    for k in range(6):
+        far_copy(k).wait_send()
+    for i in range(2):
+        leg1_copy(i).wait_send()
+        leg2_copy(i).wait_send()
+    for c in halo_copies(cg3, cg_halo, ch_send, ch_recv):
+        c.wait_send()
+
     for p in PART_ORDER:
         s1_finish(p)
+
+    for p in PART_ORDER:
+        s2_finish(p)
 
     back_b[high] = collect(back_a, 8, low, low_of, ba_send, ba_recv)
     exchange(back_b, 16, high, high_of, bb_send, bb_recv)
 
     for p in PART_ORDER:
-        s2_finish(p)
+        core_copy(p).wait_send()
+        loop3(first_axis(p)[0], lambda o: s1_copy(p, o).wait_send())
+    drain(back_a, 8, low, low_of, ba_send, ba_recv)
+
+    def quarter_at(p, first):
+        return pl.multiple_of(p * PART + QUARTER * first, QUARTER)
+
+    def shard_at(p, first, second):
+        return pl.multiple_of(p * PART + QUARTER * first + SHARD * second, SHARD)
+
+    def own_shard(p):
+        return full.at[core, pl.ds(shard_at(p, first_axis(p)[0], second_axis(p)[0]), SHARD)]
+
+    def g3_copy(p, o):
+        rows = own_shard(p)
+        return copy(rows, rows, g3_send.at[o], g3_recv.at[p], at_zh(o))
+
+    def g2_copy(p, o, sender):
+        rows = full.at[core, pl.ds(shard_at(p, first_axis(p)[0], sender), SHARD)]
+        return copy(rows, rows, g2_send.at[p, o], g2_recv.at[p, sender], second_axis(p)[1](o))
+
+    def g1_copy(p, o, sender):
+        rows = full.at[core, pl.ds(quarter_at(p, sender), QUARTER)]
+        return copy(rows, rows, g1_send.at[p, o], g1_recv.at[p, sender], first_axis(p)[1](o))
+
+    def to_core(p, half):
+        rows = full.at[half, pl.ds(p * PART, PART)]
+        return copy(rows, rows, gc_send.at[p], gc_recv.at[p], at(other_core))
+
+    def store_params(p, half, slot):
+        rows = pl.ds(p * PART, PART)
+        return pltpu.make_async_copy(
+            full.at[half, rows], params_out.at[half, rows], store_sem.at[1 + slot * PARTS + p]
+        )
+
+    for p in PART_ORDER:
+        @pl.when(zh == p)
+        def finish_part():
+            in3[z] = mid2[p]
+
+            def arrived(j, _):
+                o = lax.rem(z + j, 8)
+                copy(in3.at[o], in3.at[o], s3_send.at[o], s3_recv.at[o], at_z(o)).wait_recv()
+                return 0
+
+            lax.fori_loop(1, 8, arrived, 0)
+            total = in3[0]
+            for o in range(1, 8):
+                total = total + in3[o]
+            where = pl.ds(shard_at(p, first_axis(p)[0], second_axis(p)[0]), SHARD)
+            full[core, where, :] = (total * SCALE).astype(BF16)
+            loop3(zh, lambda o: g3_copy(p, o).start())
+
+    for p in PART_ORDER:
+        @pl.when(zh != p)
+        def take_part():
+            g3_copy(p, zh + 1 - 2 * lax.rem(zh, 2)).wait_recv()
+
+        me, _ = second_axis(p)
+        loop3(me, lambda o: g2_copy(p, o, me).start())
+
+    for p in PART_ORDER:
+        loop3(second_axis(p)[0], lambda o: s2_copy(p, o).wait_send())
+
+    for p in PART_ORDER:
+        loop3(second_axis(p)[0], lambda o: g2_copy(p, o, o).wait_recv())
+        me, _ = first_axis(p)
+        loop3(me, lambda o: g1_copy(p, o, me).start())
 
     sums = collect(back_b, 16, high, high_of, bb_send, bb_recv)
     clip_sums[clip] = sums
@@ -533,117 +623,41 @@
     store_grad = pltpu.make_async_copy(grad_v, grad_out, store_sem.at[0])
     store_grad.start()
 
-    def quarter_at(p, first):
-        return pl.multiple_of(p * PART + QUARTER * first, QUARTER)
-
-    def shard_at(p, first, second):
-        return pl.multiple_of(p * PART + QUARTER * first + SHARD * second, SHARD)
-
-    def own_shard(p):
-        return full.at[core, pl.ds(shard_at(p, first_axis(p)[0], second_axis(p)[0]), SHARD)]
-
-    def g3_copy(p, o):
-        rows = own_shard(p)
-        return copy(rows, rows, g3_send.at[o], g3_recv.at[p], at_zh(o))
-
-    def g2_copy(p, o, sender):
-        rows = full.at[core, pl.ds(shard_at(p, first_axis(p)[0], sender), SHARD)]
-        return copy(rows, rows, g2_send.at[p, o], g2_recv.at[p, sender], second_axis(p)[1](o))
-
-    def g1_copy(p, o, sender):
-        rows = full.at[core, pl.ds(quarter_at(p, sender), QUARTER)]
-        return copy(rows, rows, g1_send.at[p, o], g1_recv.at[p, sender], first_axis(p)[1](o))
-
-    def to_core(p, half):
-        rows = full.at[half, pl.ds(p * PART, PART)]
-        return copy(rows, rows, gc_send.at[p], gc_recv.at[p], at(other_core))
-
-    def store_params(p, half, slot):
-        rows = pl.ds(p * PART, PART)
-        return pltpu.make_async_copy(
-            full.at[half, rows], params_out.at[half, rows], store_sem.at[1 + slot * PARTS + p]
-        )
-
+    def s3_sent(j, _):
+        s3_copy(lax.rem(z + j, 8), z).wait_send()
+        return 0
+
+    lax.fori_loop(1, 8, s3_sent, 0)
+    drain(back_b, 16, high, high_of, bb_send, bb_recv)
     for p in PART_ORDER:
         @pl.when(zh == p)
-        def finish_part():
-            in3[z] = mid2[p]
-
-            def arrived(j, _):
-                o = lax.rem(z + j, 8)
-                copy(in3.at[o], in3.at[o], s3_send.at[o], s3_recv.at[o], at_z(o)).wait_recv()
-                return 0
-
-            lax.fori_loop(1, 8, arrived, 0)
-            total = in3[0]
-            for o in range(1, 8):
-                total = total + in3[o]
-            where = pl.ds(shard_at(p, first_axis(p)[0], second_axis(p)[0]), SHARD)
-            full[core, where, :] = (total * SCALE).astype(BF16)
-            loop3(zh, lambda o: g3_copy(p, o).start())
-
-        @pl.when(zh != p)
-        def take_part():
-            g3_copy(p, zh + 1 - 2 * lax.rem(zh, 2)).wait_recv()
-
-        me, _ = second_axis(p)
-        loop3(me, lambda o: g2_copy(p, o, me).start())
-
+        def sent_part():
+            loop3(zh, lambda o: g3_copy(p, o).wait_send())
+
+        loop3(second_axis(p)[0], lambda o: g2_copy(p, o, second_axis(p)[0]).wait_send())
+
+    for p in PART_ORDER:
+        loop3(first_axis(p)[0], lambda o: g1_copy(p, o, o).wait_recv())
+        to_core(p, core).start()
+        store_params(p, core, 0).start()
+
+    for p in PART_ORDER:
+        loop3(first_axis(p)[0], lambda o: g1_copy(p, o, first_axis(p)[0]).wait_send())
+
+    for p in PART_ORDER:
+        to_core(p, 1 - core).wait_recv()
+        store_params(p, 1 - core, 1).start()
     copy(
         clip_sums.at[1 - clip], clip_sums.at[1 - clip], clip_sem.at[0], clip_sem.at[1],
         (1 - clip, seq),
     ).wait_recv()
-    both = (clip_sums[0] + clip_sums[1]) * SCALE
-    bias_out[...] = both[0:1]
-    gain_out[...] = both[1:2]
-
-    for p in PART_ORDER:
-        loop3(second_axis(p)[0], lambda o: g2_copy(p, o, o).wait_recv())
-        me, _ = first_axis(p)
-        loop3(me, lambda o: g1_copy(p, o, me).start())
-
-    for p in PART_ORDER:
-        loop3(first_axis(p)[0], lambda o: g1_copy(p, o, o).wait_recv())
-        to_core(p, core).start()
-        store_params(p, core, 0).start()
-
-    for k in range(8):
-        near_copy(k, True).wait_send()
-    for k in range(6):
-        far_copy(k).wait_send()
-    for i in range(2):
-        leg1_copy(i).wait_send()
-        leg2_copy(i).wait_send()
-    for args in ((act3, act_halo, ah_send, ah_recv), (cg3, cg_halo, ch_send, ch_recv)):
-        for c in halo_copies(*args):
-            c.wait_send()
-    drain(stat_a, 8, low, low_of, sa_send, sa_recv)
-    drain(stat_b, 16, high, high_of, sb_send, sb_recv)
-    drain(back_a, 8, low, low_of, ba_send, ba_recv)
-    drain(back_b, 16, high, high_of, bb_send, bb_recv)
+    sums_v[...] = (clip_sums[0] + clip_sums[1]) * SCALE
+    store_sums = pltpu.make_async_copy(sums_v, sums_out, store_sem.at[1 + 2 * PARTS])
+    store_sums.start()
+
     clip_copy.wait_send()
-
-    def s3_sent(j, _):
-        s3_copy(lax.rem(z + j, 8), z).wait_send()
-        return 0
-
-    lax.fori_loop(1, 8, s3_sent, 0)
-    for p in range(PARTS):
-        @pl.when(zh == p)
-        def sent_part():
-            loop3(zh, lambda o: g3_copy(p, o).wait_send())
-
-    for p in range(PARTS):
-        core_copy(p).wait_send()
-        loop3(first_axis(p)[0], lambda o: s1_copy(p, o).wait_send())
-        loop3(second_axis(p)[0], lambda o: s2_copy(p, o).wait_send())
-        loop3(second_axis(p)[0], lambda o: g2_copy(p, o, second_axis(p)[0]).wait_send())
-        loop3(first_axis(p)[0], lambda o: g1_copy(p, o, first_axis(p)[0]).wait_send())
-
-    for p in PART_ORDER:
-        to_core(p, 1 - core).wait_recv()
-        store_params(p, 1 - core, 1).start()
     store_grad.wait()
+    store_sums.wait()
     for p in PART_ORDER:
         to_core(p, core).wait_send()
         store_params(p, core, 0).wait()
@@ -651,10 +665,11 @@
 
 
 def finish_kernel(
-    grad, params, gain, bias, grad_out, spatial, temporal, gain_out, bias_out,
-    params_v, out_v, sem,
+    grad, params, sums, grad_out, spatial, temporal, gain_out, bias_out,
+    grad_v, params_v, out_v, sums_v, bias_v, gain_v, sem,
 ):
-    move_grad = pltpu.make_async_copy(grad, grad_out, sem.at[0])
+    load_grad = pltpu.make_async_copy(grad, grad_v, sem.at[0])
+    store_grad = pltpu.make_async_copy(grad_v, grad_out, sem.at[9])
 
     def load(i):
         taps = pl.ds(3 * i, 3)
@@ -666,9 +681,11 @@
 
     for i in range(4):
         load(i).start()
-    move_grad.start()
-    gain_out[...] = gain[0]
-    bias_out[...] = bias[0]
+    load_grad.start()
+    load_sums = pltpu.make_async_copy(sums, sums_v, sem.at[10])
+    load_sums.start()
+    store_bias = pltpu.make_async_copy(bias_v, bias_out, sem.at[11])
+    store_gain = pltpu.make_async_copy(gain_v, gain_out, sem.at[12])
     for i in range(4):
         load(i).wait()
         for half in range(2):
@@ -676,14 +693,22 @@
                 half, 3 * i : 3 * i + 3
             ].astype(F32)
         store(i).start()
-    move_grad.wait()
+    load_grad.wait()
+    store_grad.start()
+    load_sums.wait()
+    bias_v[...] = sums_v[0]
+    gain_v[...] = sums_v[1]
+    store_bias.start()
+    store_gain.start()
+    store_grad.wait()
+    store_bias.wait()
+    store_gain.wait()
     for i in range(4):
         store(i).wait()
 
 
 def local(block_input, cotangent, group_norm_gain, group_norm_bias, w_spatial, w_temporal):
     any_space = pl.BlockSpec(memory_space=pl.ANY)
-    vmem = pl.BlockSpec(memory_space=pltpu.VMEM)
     dma = pltpu.SemaphoreType.DMA
     scratch = [
         pltpu.VMEM((PIXELS, CHANNELS), BF16),
@@ -714,7 +739,9 @@
         pltpu.VMEM((2, HALF_ROWS, 128), BF16),
         pltpu.VMEM((PIXELS, CHANNELS), BF16),
         pltpu.VMEM((2, COLS, CHANNELS), BF16),
-        dma((4,)), dma((1 + 2 * PARTS,)),
+        pltpu.VMEM((2, 1, CHANNELS), F32),
+        pltpu.VMEM((8, CHANNELS), F32),
+        dma((6,)), dma((2 + 2 * PARTS,)),
         dma((8,)), dma((8,)), dma((8,)), dma((8,)),
         dma((2,)), dma((2,)), dma((2,)),
         dma((2,)), dma((2,)), dma((2,)), dma((2,)),
@@ -727,16 +754,15 @@
         dma((4,)), dma((4,)), dma((4, 4)), dma((4, 4)), dma((4, 4)), dma((4, 4)),
         dma((4,)), dma((4,)),
     ]
-    grad, params, gain_grad, bias_grad = pl.pallas_call(
+    grad, params, sums = pl.pallas_call(
         kernel,
         out_shape=(
             jax.ShapeDtypeStruct((PIXELS, CHANNELS), BF16),
             jax.ShapeDtypeStruct((2, HALF_ROWS, 128), BF16),
-            jax.ShapeDtypeStruct((1, CHANNELS), F32),
-            jax.ShapeDtypeStruct((1, CHANNELS), F32),
+            jax.ShapeDtypeStruct((8, CHANNELS), F32),
         ),
-        in_specs=[any_space, any_space, vmem, vmem, any_space, any_space],
-        out_specs=(any_space, any_space, vmem, vmem),
+        in_specs=[any_space] * 6,
+        out_specs=(any_space, any_space, any_space),
         scratch_shapes=scratch,
         compiler_params=pltpu.CompilerParams(
             collective_id=0, has_side_effects=True, vmem_limit_bytes=56 * 2**20
@@ -759,15 +785,19 @@
             jax.ShapeDtypeStruct((CHANNELS,), F32),
             jax.ShapeDtypeStruct((CHANNELS,), F32),
         ),
-        in_specs=[any_space, any_space, vmem, vmem],
-        out_specs=(any_space, any_space, any_space, vmem, vmem),
+        in_specs=[any_space] * 3,
+        out_specs=(any_space,) * 5,
         scratch_shapes=[
+            pltpu.VMEM((PIXELS, CHANNELS), BF16),
             pltpu.VMEM((2, TAPS, CHANNELS, 128), BF16),
             pltpu.VMEM((TAPS, CHANNELS, CHANNELS), F32),
-            dma((9,)),
+            pltpu.VMEM((8, CHANNELS), F32),
+            pltpu.VMEM((CHANNELS,), F32),
+            pltpu.VMEM((CHANNELS,), F32),
+            dma((13,)),
         ],
         compiler_params=pltpu.CompilerParams(vmem_limit_bytes=60 * 2**20),
-    )(grad, params, gain_grad, bias_grad)
+    )(grad, params, sums)
     return (
         grad.reshape(1, ROWS_DEV, COLS, CHANNELS),
         spatial,

time: 126 us -> 95.3 us (0.76)
  Pallas kernels: 126 us -> 94.5 us
    pallas_call x1, Pallas kernels: 22.3 us -> 3.05 us  [local(): pl.pallas_call(finish_kernel, out_shape=(jax.ShapeDtypeStruct((PIXELS, CH...]
    pallas_call x1, Pallas kernels: 103 us -> 91.5 us  [local(): pl.pallas_call(kernel, out_shape=(jax.ShapeDtypeStruct((PIXELS, CHANNELS)...]
where the time goes in v5:
time: 95.3 us; the launch traced here: 95.1 us
  Pallas kernels  94.5 us (99%)
    pallas_call x1, Pallas kernels, local(): pl.pallas_call(kernel, out_shape=(jax.ShapeDtypeStruct((PIXELS, CHANNELS)...  91.5 us
    pallas_call x1, Pallas kernels, local(): pl.pallas_call(finish_kernel, out_shape=(jax.ShapeDtypeStruct((PIXELS, CH...  3.05 us

profile of v5, /device:TPU:1, one launch (start us, length us, event | category | flops | bytes accessed | tf_op | source)
XLA Modules:
  0.0 95.1 jit_solution(15296043035223704094)
XLA Ops:
  0.6 91.5 %shard_map.101 = (bf16[1280,256]{1,0:T(8,128)(2,1)}, bf16[2,3072,128]{2,1,0:T(8,128)(2,1)}, f32[8,256]{1,0:T(8,128)}) custom-call(bf16[1280,256]{1,0:T(8,128)(2,1)} %bitcast.9, bf16[1280,256]{1,0:T(8,128)(2,1)} %bitcast.10, f32[1,256]{1,0:T(1,128)} %bitcast.11, f32[1,256]{1,0:T(1,128)} %bitcast.12, bf16[2304,256]{1,0:T(8,128)(2,1)} %bitcast.8, ...), custom_call_target="tpu_custom_call" | custom-call | tf_op jit(solution)/shard_map/pallas_call | solution.py:757
  92.1 3.0 %shard_map.102 = (bf16[1280,256]{1,0:T(8,128)(2,1)}, f32[9,256,256]{2,1,0:T(8,128)}, f32[3,256,256]{2,1,0:T(8,128)}, f32[256]{0:T(256)}, f32[256]{0:T(256)}) custom-call(bf16[1280,256]{1,0:T(8,128)(2,1)} %get-tuple-element.13.grad, bf16[2,12,256,128]{3,2,1,0:T(8,128)(2,1)} %bitcast.7, f32[8,256]{1,0:T(8,128)} %get-tuple-element.15.sums), custom_call_target="tpu_custom_call" | custom-call | tf_op jit(solution)/shard_map/pallas_call | solution.py:779

commit v6 on v5

--- a/solution.py
+++ b/solution.py
@@ -201,10 +201,10 @@
     def high_of(o):
         return o * 8 + low
 
-    row_id = lax.broadcasted_iota(jnp.int32, (8, CHANNELS), 0)
+    row_id = lax.broadcasted_iota(jnp.int32, (2, CHANNELS), 0)
 
     def pack_rows(first, second):
-        return jnp.where(row_id == 0, first, jnp.where(row_id == 1, second, 0.0))
+        return jnp.where(row_id == 0, first, second)
 
     group_a = lax.shift_right_logical(lax.broadcasted_iota(jnp.int32, (CHANNELS, CHANNELS), 0), 3)
     group_b = lax.shift_right_logical(lax.broadcasted_iota(jnp.int32, (CHANNELS, CHANNELS), 1), 3)
@@ -387,10 +387,11 @@
     forward(0)
     pass_detour(1)
     forward(1)
+    forward(2)
     cg_row(0)
     cg_row(1)
     send_halo(cg3, cg_halo, ch_send, ch_recv)
-    forward(2)
+    forward(3)
     take_halo(act3, act_halo, ah_send, ah_recv)
 
     def conv_body(i, _):
@@ -398,7 +399,8 @@
         return 0
 
     lax.fori_loop(0, PIXELS // BLOCK, conv_body, 0)
-    forward(3)
+    forward(4)
+    cg_row(2)
 
     def turn_conv(i, _):
         src = pl.ds(pl.multiple_of(i * 128, 128), 128)
@@ -406,23 +408,22 @@
         return 0
 
     lax.fori_loop(0, PIXELS // 128, turn_conv, 0)
-    cg_row(2)
-    forward(4)
     cg_row(3)
+    forward(5)
+    cg_row(4)
+    forward(6)
+    temporal_half(0)
+    spatial_half(0, 0)
+    forward(7)
+    spatial_half(0, 1)
+    spatial_half(0, 2)
     drain(stat_a, 8, low, low_of, sa_send, sa_recv)
     drain(stat_b, 16, high, high_of, sb_send, sb_recv)
     for c in halo_copies(act3, act_halo, ah_send, ah_recv):
         c.wait_send()
-    forward(5)
-    cg_row(4)
-    temporal_half(0)
-    for dy in range(3):
-        spatial_half(0, dy)
-    forward(6)
     cg_row(5)
-    forward(7)
+    take_halo(cg3, cg_halo, ch_send, ch_recv)
     cg_row(6)
-    take_halo(cg3, cg_halo, ch_send, ch_recv)
     cg_row(7)
     temporal_half(1)
     core_copy(3).start()
@@ -724,11 +725,11 @@
         pltpu.VMEM((PIXELS, CHANNELS), F32),
         pltpu.VMEM((2, COLS, CHANNELS), BF16),
         pltpu.VMEM((2, COLS, CHANNELS), BF16),
-        pltpu.VMEM((8, 8, CHANNELS), F32),
-        pltpu.VMEM((16, 8, CHANNELS), F32),
-        pltpu.VMEM((8, 8, CHANNELS), F32),
-        pltpu.VMEM((16, 8, CHANNELS), F32),
-        pltpu.VMEM((2, 8, CHANNELS), F32),
+        pltpu.VMEM((8, 2, CHANNELS), F32),
+        pltpu.VMEM((16, 2, CHANNELS), F32),
+        pltpu.VMEM((8, 2, CHANNELS), F32),
+        pltpu.VMEM((16, 2, CHANNELS), F32),
+        pltpu.VMEM((2, 2, CHANNELS), F32),
         pltpu.VMEM((2, HALF_ROWS, 128), F32),
         pltpu.VMEM((HALF_ROWS, 128), F32),
         pltpu.VMEM((PARTS, 4, QUARTER, 128), F32),
@@ -740,7 +741,7 @@
         pltpu.VMEM((PIXELS, CHANNELS), BF16),
         pltpu.VMEM((2, COLS, CHANNELS), BF16),
         pltpu.VMEM((2, 1, CHANNELS), F32),
-        pltpu.VMEM((8, CHANNELS), F32),
+        pltpu.VMEM((2, CHANNELS), F32),
         dma((6,)), dma((2 + 2 * PARTS,)),
         dma((8,)), dma((8,)), dma((8,)), dma((8,)),
         dma((2,)), dma((2,)), dma((2,)),
@@ -759,7 +760,7 @@
         out_shape=(
             jax.ShapeDtypeStruct((PIXELS, CHANNELS), BF16),
             jax.ShapeDtypeStruct((2, HALF_ROWS, 128), BF16),
-            jax.ShapeDtypeStruct((8, CHANNELS), F32),
+            jax.ShapeDtypeStruct((2, CHANNELS), F32),
         ),
         in_specs=[any_space] * 6,
         out_specs=(any_space, any_space, any_space),
@@ -791,7 +792,7 @@
             pltpu.VMEM((PIXELS, CHANNELS), BF16),
             pltpu.VMEM((2, TAPS, CHANNELS, 128), BF16),
             pltpu.VMEM((TAPS, CHANNELS, CHANNELS), F32),
-            pltpu.VMEM((8, CHANNELS), F32),
+            pltpu.VMEM((2, CHANNELS), F32),
             pltpu.VMEM((CHANNELS,), F32),
             pltpu.VMEM((CHANNELS,), F32),
             dma((13,)),

time: 95.3 us -> 92.4 us (0.970)
  Pallas kernels: 94.5 us -> 91.6 us
    pallas_call x1, Pallas kernels: 91.5 us -> 88.5 us  [local(): pl.pallas_call(kernel, out_shape=(jax.ShapeDtypeStruct((PIXELS, CHANNELS)...]
where the time goes in v6:
time: 92.4 us; the launch traced here: 92.2 us
  Pallas kernels  91.6 us (99%)
    pallas_call x1, Pallas kernels, local(): pl.pallas_call(kernel, out_shape=(jax.ShapeDtypeStruct((PIXELS, CHANNELS)...  88.5 us
    pallas_call x1, Pallas kernels, local(): pl.pallas_call(finish_kernel, out_shape=(jax.ShapeDtypeStruct((PIXELS, CH...  3.05 us

profile of v6, /device:TPU:1, one launch (start us, length us, event | category | flops | bytes accessed | tf_op | source)
XLA Modules:
  0.0 92.2 jit_solution(9356797660893555463)
XLA Ops:
  0.6 88.5 %shard_map.101 = (bf16[1280,256]{1,0:T(8,128)(2,1)}, bf16[2,3072,128]{2,1,0:T(8,128)(2,1)}, f32[2,256]{1,0:T(2,128)}) custom-call(bf16[1280,256]{1,0:T(8,128)(2,1)} %bitcast.9, bf16[1280,256]{1,0:T(8,128)(2,1)} %bitcast.10, f32[1,256]{1,0:T(1,128)} %bitcast.11, f32[1,256]{1,0:T(1,128)} %bitcast.12, bf16[2304,256]{1,0:T(8,128)(2,1)} %bitcast.8, ...), custom_call_target="tpu_custom_call" | custom-call | tf_op jit(solution)/shard_map/pallas_call | solution.py:758
  89.2 3.0 %shard_map.102 = (bf16[1280,256]{1,0:T(8,128)(2,1)}, f32[9,256,256]{2,1,0:T(8,128)}, f32[3,256,256]{2,1,0:T(8,128)}, f32[256]{0:T(256)}, f32[256]{0:T(256)}) custom-call(bf16[1280,256]{1,0:T(8,128)(2,1)} %get-tuple-element.13.grad, bf16[2,12,256,128]{3,2,1,0:T(8,128)(2,1)} %bitcast.7, f32[2,256]{1,0:T(2,128)} %get-tuple-element.15.sums), custom_call_target="tpu_custom_call" | custom-call | tf_op jit(solution)/shard_map/pallas_call | solution.py:780

commit v7 on v6

--- a/solution.py
+++ b/solution.py
@@ -483,9 +483,11 @@
         loop3(first_axis(p)[0], lambda o: s1_copy(p, o).start())
 
     sums = (zero8, zero8)
-    for i, p in enumerate(PART_ORDER):
+    add_core(PART_ORDER[0])
+    for i, p in enumerate(PART_ORDER[1:]):
+        add_core(p)
         sums = back_block(i, sums)
-        add_core(p)
+    sums = back_block(PARTS - 1, sums)
     a, b = sums
     back_a[low] = pack_rows(jnp.sum(a, axis=0, keepdims=True), jnp.sum(b, axis=0, keepdims=True))
     exchange(back_a, 8, low, low_of, ba_send, ba_recv)

time: 92.4 us -> 92.5 us (level)
  no operation moved by 1% of the time
where the time goes in v7:
time: 92.5 us; the launch traced here: 92.3 us
  Pallas kernels  91.7 us (99%)
    pallas_call x1, Pallas kernels, local(): pl.pallas_call(kernel, out_shape=(jax.ShapeDtypeStruct((PIXELS, CHANNELS)...  88.6 us
    pallas_call x1, Pallas kernels, local(): pl.pallas_call(finish_kernel, out_shape=(jax.ShapeDtypeStruct((PIXELS, CH...  3.05 us

profile of v7, /device:TPU:1, one launch (start us, length us, event | category | flops | bytes accessed | tf_op | source)
XLA Modules:
  0.0 92.3 jit_solution(13093924067140632060)
XLA Ops:
  0.6 88.6 %shard_map.101 = (bf16[1280,256]{1,0:T(8,128)(2,1)}, bf16[2,3072,128]{2,1,0:T(8,128)(2,1)}, f32[2,256]{1,0:T(2,128)}) custom-call(bf16[1280,256]{1,0:T(8,128)(2,1)} %bitcast.9, bf16[1280,256]{1,0:T(8,128)(2,1)} %bitcast.10, f32[1,256]{1,0:T(1,128)} %bitcast.11, f32[1,256]{1,0:T(1,128)} %bitcast.12, bf16[2304,256]{1,0:T(8,128)(2,1)} %bitcast.8, ...), custom_call_target="tpu_custom_call" | custom-call | tf_op jit(solution)/shard_map/pallas_call | solution.py:760
  89.3 3.0 %shard_map.102 = (bf16[1280,256]{1,0:T(8,128)(2,1)}, f32[9,256,256]{2,1,0:T(8,128)}, f32[3,256,256]{2,1,0:T(8,128)}, f32[256]{0:T(256)}, f32[256]{0:T(256)}) custom-call(bf16[1280,256]{1,0:T(8,128)(2,1)} %get-tuple-element.13.grad, bf16[2,12,256,128]{3,2,1,0:T(8,128)(2,1)} %bitcast.7, f32[2,256]{1,0:T(2,128)} %get-tuple-element.15.sums), custom_call_target="tpu_custom_call" | custom-call | tf_op jit(solution)/shard_map/pallas_call | solution.py:782
